TPU v7x, 128 devices: a whole 4x4x4 slice. The times are simulated.
128 devices in a mesh: phase: 8 (over x, core), tp: 16 (over z, y).
Axes of the slice: x: 4, y: 4, z: 4, core: 2. Of those that a mesh axis runs over, the one named last changes fastest.
Arguments:
- teacher_rows: bfloat16 [512, 16384], P(None, ('phase', 'tp')), may hold values from -128 to 128
- teacher_gain: bfloat16 [16384], P(('phase', 'tp')), may hold values from 0.25 to 1.75
- teacher_head: bfloat16 [16384, 65536], P(None, ('phase', 'tp')), may hold values from -1 to 1
- student_rows: bfloat16 [512, 4096], P('phase', 'tp'), may hold values from -128 to 128
- student_gain: bfloat16 [4096], P('tp'), may hold values from 0.25 to 1.75
- student_head: bfloat16 [4096, 65536], P(None, ('phase', 'tp')), may hold values from -1 to 1
- labels: int32 [512], replicated, may hold values from 0 to 65535
Outputs:
- token_loss: float32 [512], P('phase')
- student_head_grad: bfloat16 [4096, 65536], P(None, ('phase', 'tp'))
- student_rows_grad: bfloat16 [512, 4096], P('phase', 'tp')
- student_gain_grad: float32 [4096], P('tp')
All inputs are finite; a program needn't handle non-finite values.
Results may differ from a plain program's by a relative error of at most 0.011.
Values may be sent and summed in bfloat16 or wider, within the bound.
A program may use at most 128 MiB of HBM per device.

v0:
```python
import jax
import jax.numpy as jnp
from jax import lax
from jax.sharding import PartitionSpec as P

NORM_EPSILON = 1e-05
LABEL_WEIGHT = 0.5


def local(
    teacher_rows, teacher_gain, teacher_head, student_rows, student_gain, student_head, labels
):
    tp_count = lax.axis_size("tp")
    phase_pos = lax.axis_index("phase")
    tp_pos = lax.axis_index("tp")
    vocab_local = teacher_head.shape[1]
    slab_rows = student_rows.shape[0]
    teacher_span = teacher_head.shape[0]
    student_span = student_head.shape[0]
    teacher_wide = teacher_rows.astype(jnp.float32)
    teacher_squares = lax.psum(jnp.sum(teacher_wide * teacher_wide, axis=1), ("phase", "tp"))
    teacher_scale = lax.rsqrt(teacher_squares / teacher_span + NORM_EPSILON)
    teacher_scaled = (teacher_wide * teacher_gain.astype(jnp.float32)).astype(jnp.bfloat16)
    head_rows = teacher_head
    raw_logits = jnp.dot(
        lax.all_gather(teacher_scaled, ("phase", "tp"), axis=1, tiled=True),
        head_rows,
        preferred_element_type=jnp.float32,
    )
    teacher_logits = teacher_scale[:, None] * raw_logits
    student_wide = student_rows.astype(jnp.float32)
    gain_wide = student_gain.astype(jnp.float32)
    phase_rows = lax.all_gather(student_rows, "phase", axis=0, tiled=True)
    full_rows, full_gain = (
        lax.all_gather(phase_rows, "tp", axis=1, tiled=True),
        lax.all_gather(student_gain, "tp", axis=0, tiled=True),
    )
    full_wide = full_rows.astype(jnp.float32)
    full_scale = lax.rsqrt(jnp.mean(full_wide * full_wide, axis=1) + NORM_EPSILON)
    student_normed = (full_wide * full_scale[:, None] * full_gain.astype(jnp.float32)).astype(
        jnp.bfloat16
    )
    student_scale = lax.dynamic_slice_in_dim(full_scale, phase_pos * slab_rows, slab_rows, 0)
    student_logits = jnp.dot(student_normed, student_head, preferred_element_type=jnp.float32)
    vocab_first = (phase_pos * tp_count + tp_pos) * vocab_local
    label_hit = labels[:, None] == (vocab_first + jnp.arange(vocab_local, dtype=jnp.int32))[None, :]
    picked_local = jnp.sum(jnp.where(label_hit, student_logits, 0.0), axis=1)
    teacher_top, student_top = lax.pmax(
        (jnp.max(teacher_logits, axis=1), jnp.max(student_logits, axis=1)), ("phase", "tp")
    )
    teacher_exp = jnp.exp(teacher_logits - teacher_top[:, None])
    teacher_total, teacher_cross, student_total, picked = lax.psum(
        (
            jnp.sum(teacher_exp, axis=1),
            jnp.sum(teacher_exp * (teacher_logits - student_logits), axis=1),
            jnp.sum(jnp.exp(student_logits - student_top[:, None]), axis=1),
            picked_local,
        ),
        ("phase", "tp"),
    )
    teacher_lse = teacher_top + jnp.log(teacher_total)
    student_lse = student_top + jnp.log(student_total)
    every_loss = (
        teacher_cross / teacher_total
        - teacher_lse
        + student_lse
        + LABEL_WEIGHT * (student_lse - picked)
    )
    token_loss = lax.dynamic_slice_in_dim(every_loss, phase_pos * slab_rows, slab_rows, 0)
    teacher_prob = jnp.exp(teacher_logits - teacher_top[:, None]) / teacher_total[:, None]
    student_prob = jnp.exp(student_logits - student_lse[:, None])
    logit_grad = (
        (1.0 + LABEL_WEIGHT) * student_prob
        - teacher_prob
        - LABEL_WEIGHT * label_hit.astype(jnp.float32)
    ).astype(jnp.bfloat16)
    head_grad = lax.dot_general(
        student_normed, logit_grad, (((0,), (0,)), ((), ())), preferred_element_type=jnp.float32
    ).astype(jnp.bfloat16)
    head_rows = student_head
    width_part = lax.psum_scatter(
        lax.dot_general(
            head_rows, logit_grad, (((1,), (1,)), ((), ())), preferred_element_type=jnp.float32
        ),
        "tp",
        scatter_dimension=0,
        tiled=True,
    )
    own_columns = lax.psum_scatter(width_part, "phase", scatter_dimension=1, tiled=True)
    normed_grad = jnp.transpose(own_columns)
    norm_inner = lax.psum(jnp.sum(gain_wide * normed_grad * student_wide, axis=1), "tp")
    cubed = student_scale * student_scale * student_scale
    rows_grad = (
        student_scale[:, None] * gain_wide * normed_grad
        - student_wide * cubed[:, None] * norm_inner[:, None] / student_span
    ).astype(jnp.bfloat16)
    gain_grad = lax.psum(
        jnp.sum(normed_grad * student_wide * student_scale[:, None], axis=0), "phase"
    )
    return (token_loss, head_grad, rows_grad, gain_grad)


def solution(mesh):
    placed = (
        P(None, ("phase", "tp")),
        P(("phase", "tp")),
        P(None, ("phase", "tp")),
        P("phase", "tp"),
        P("tp"),
        P(None, ("phase", "tp")),
        P(),
    )
    return jax.shard_map(
        local,
        mesh=mesh,
        in_specs=placed,
        out_specs=(P("phase"), P(None, ("phase", "tp")), P("phase", "tp"), P("tp")),
        check_vma=False,
    )
```

profile of v0, /device:TPU:1, one launch (start us, length us, event | category | flops | bytes accessed | tf_op | source)
XLA Modules:
  0.0 515.5 jit_solution(17956571211534801297)
XLA Ops:
  7.2 0.0 all-gather.6.cloned.1.call-start
  7.2 15.8 %all_gather.13 = bf16[512,256]{1,0:T(8,128)(2,1)} all-gather(bf16[64,256]{1,0:T(8,128)(2,1)} %param.10), channel_id=1, replica_groups=mesh['phase'=8,'tp'=16] {'phase'}, dimensions={0}, use_global_device_ids=true | all-gather | bytes 294912 | tf_op jit(solution)/shard_map/all_gather | solution.py:33
  23.0 0.0 all-gather.6.cloned.1.call-update
  23.1 0.0 all-gather.4.cloned.1.call-start
  23.1 0.7 convert_element_type.35
  23.8 1.6 fusion.10
  25.4 0.0 all-gather.4.cloned.1.call-update
  25.4 0.0 reduce-scatter.3.cloned.1.call-start
  25.4 0.7 reshape.29
  26.1 20.1 %all-gather = bf16[16,1,256]{2,1,0:T(2,128)(2,1)S(1)} all-gather(bf16[1,1,256]{2,1,0:T(2,128)(2,1)S(1)} %reshape.29), channel_id=1, replica_groups=mesh['phase'=8,'tp'=16] {'tp'}, dimensions={0}, use_global_device_ids=true | all-gather | bytes 8704 | tf_op jit(solution)/shard_map/all_gather | solution.py:36
  46.2 68.6 %psum.49 = f32[512]{0:T(512)S(1)} all-reduce(f32[512]{0:T(512)S(1)} %get-tuple-element.20), channel_id=1, replica_groups=mesh['phase'=8,'tp'=16] {'phase','tp'}, use_global_device_ids=true, to_apply=%region_1.0 | all-reduce | flops 512 | bytes 4096 | tf_op jit(solution)/shard_map/psum | solution.py:21
  114.8 0.0 all-gather.6.cloned.1.call-done
  114.9 3.1 fusion
  118.0 5.9 %fusion.19 = (f32[512]{0:T(512)S(1)}, f32[512,512]{0,1:T(8,128)S(1)}) fusion(bf16[4096,512]{1,0:T(8,128)(2,1)} %param.12, bf16[512,4096]{1,0:T(8,128)(2,1)} %all-gather.6.cloned.1.call-done, f32[4096]{0:T(1024)S(1)} %bitcast.15, f32[512]{0:T(512)S(1)} %add_rsqrt_fusion), kind=kOutput, calls=%fused_computation.40 | convolution fusion | flops 2156133888 | bytes 9457664 | tf_op jit(solution)/shard_map/dot_general | solution.py:44
  124.0 0.0 copy-start.1
  124.0 63.0 %all-gather.4.cloned.1.call-done = bf16[512,16384]{1,0:T(8,128)(2,1)} async-done(((bf16[512,128]{1,0:T(8,128)(2,1)}), bf16[512,16384]{1,0:T(8,128)(2,1)}) %all-gather.4.cloned.1.call-update) | async-done | bytes 16777232 | tf_op jit(solution)/shard_map/all_gather | solution.py:26
  186.9 14.9 %fusion.20 = (f32[512]{0:T(512)S(1)}, f32[512,512]{0,1:T(8,128)S(1)}) fusion(bf16[512,16384]{1,0:T(8,128)(2,1)} %all-gather.4.cloned.1.call-done, bf16[16384,512]{1,0:T(8,128)(2,1)} %param.9, f32[512]{0:T(512)S(1)} %add_rsqrt_fusion.1), kind=kOutput, calls=%fused_computation.41 | convolution fusion | flops 8590458880 | bytes 34607104 | tf_op jit(solution)/shard_map/dot_general | solution.py:25
  201.8 64.6 %all-reduce.1 = (f32[512]{0:T(512)S(1)}, f32[512]{0:T(512)S(1)}) all-reduce(f32[512]{0:T(512)S(1)} %get-tuple-element.22, f32[512]{0:T(512)S(1)} %get-tuple-element.24), channel_id=1, replica_groups=mesh['phase'=8,'tp'=16] {'phase','tp'}, use_global_device_ids=true, to_apply=%region_10.11 | all-reduce | flops 1024 | bytes 8192 | tf_op jit(solution)/shard_map/pmax | solution.py:48
  266.5 0.0 copy-done.1
  266.5 0.5 multiply_reduce_fusion
  267.0 63.9 %all-reduce = (f32[512]{0:T(512)S(1)}, f32[512]{0:T(512)S(1)}, f32[512]{0:T(512)S(1)}, f32[512]{0:T(512)S(1)}) all-reduce(f32[512]{0:T(512)S(1)} %get-tuple-element.7, f32[512]{0:T(512)S(1)} %get-tuple-element.6, f32[512]{0:T(512)S(1)} %get-tuple-element.5, ...), channel_id=1, replica_groups=mesh['phase'=8,'tp'=16] {'phase','tp'}, use_global_device_ids=true, to_apply=%region_12.13 | all-reduce | flops 2048 | bytes 16384 | tf_op jit(solution)/shard_map/psum | solution.py:52
  330.9 0.0 copy-start.2
  330.9 8.1 %convolution_bitcast_fusion = f32[4096,512]{0,1:T(8,128)} fusion(bf16[4096,512]{1,0:T(8,128)(2,1)} %param.12, f32[512,512]{0,1:T(8,128)S(1)} %get-tuple-element.23, f32[512,512]{0,1:T(8,128)S(1)} %get-tuple-element.25, f32[512]{0:T(512)S(1)} %get-tuple-element.12, f32[512]{0:T(512)S(1)} %get-tuple-element.19, s32[512]{0:T(512)S(1)} %copy-done.1, ...), kind=kOutput, calls=%fused_computation.5 | convolution fusion | flops 2149842944 | bytes 14690304 | tf_op jit(solution)/shard_map/dot_general | solution.py:82
  339.0 0.0 reduce-scatter.3.cloned.1.call-update
  339.0 0.0 reduce-scatter.5.cloned.1.call-start
  339.1 80.2 %reduce-scatter.3.cloned.1.call-done = f32[256,512]{0,1:T(8,128)} async-done(((f32[4096,512]{0,1:T(8,128)}), f32[256,512]{0,1:T(8,128)}) %reduce-scatter.3.cloned.1.call-update) | async-done | bytes 524304 | tf_op jit(solution)/shard_map/reduce_scatter | solution.py:81
  419.2 0.0 reduce-scatter.5.cloned.1.call-update
  419.3 0.0 copy-done.2
  419.3 0.1 multiply_multiply_fusion
  419.4 0.6 dynamic_slice.6
  419.9 0.0 copy-start
  419.9 7.1 %convolution_convert_fusion = bf16[4096,512]{1,0:T(8,128)(2,1)} fusion(bf16[512,4096]{1,0:T(8,128)(2,1)} %all-gather.6.cloned.1.call-done, f32[4096]{0:T(1024)S(1)} %bitcast.16, f32[512]{0:T(512)S(1)} %add_rsqrt_fusion, f32[512,512]{0,1:T(8,128)S(1)} %get-tuple-element.23, f32[512,512]{0,1:T(8,128)S(1)} %get-tuple-element.25, f32[512]{0:T(512)S(1)} %get-tuple-element.12, ...), kind=kOutput, calls=%fused_computation.6 | convolution fusion | flops 2160328704 | bytes 10514432 | tf_op jit(solution)/shard_map/dot_general | solution.py:77
  427.1 23.0 %reduce-scatter.5.cloned.1.call-done = f32[256,64]{0,1:T(8,128)} async-done(((f32[256,512]{0,1:T(8,128)}), f32[256,64]{0,1:T(8,128)}) %reduce-scatter.5.cloned.1.call-update) | async-done | bytes 65552 | tf_op jit(solution)/shard_map/reduce_scatter | solution.py:89
  450.1 0.0 copy-done
  450.1 1.0 fusion.18
  451.1 33.5 %psum.54 = f32[64]{0:T(128)S(1)} all-reduce(f32[64]{0:T(128)S(1)} %get-tuple-element.9), channel_id=1, replica_groups=mesh['phase'=8,'tp'=16] {'tp'}, use_global_device_ids=true, to_apply=%region_18.19 | all-reduce | flops 64 | bytes 512 | tf_op jit(solution)/shard_map/psum | solution.py:91
  484.6 22.8 %psum.55 = f32[256]{0:T(256)} all-reduce(f32[256]{0:T(256)S(1)} %get-tuple-element.8), channel_id=1, replica_groups=mesh['phase'=8,'tp'=16] {'phase'}, use_global_device_ids=true, to_apply=%region_20.21 | all-reduce | flops 256 | bytes 2048 | tf_op jit(solution)/shard_map/psum | solution.py:97
  507.4 1.6 fusion.15
  (6 shorter events, 0.0 us)
Async XLA Ops:
  7.2 107.7 %all-gather.6.cloned.1.call-start = ((), (), s32[]{:S(2)}) async-start(), calls=%async_computation.3 | async-start | bytes 4456448 | tf_op jit(solution)/shard_map/all_gather | solution.py:35
  23.1 163.9 %all-gather.4.cloned.1.call-start = ((), (), s32[]{:S(2)}) async-start(), calls=%async_computation.2 | async-start | bytes 16908288 | tf_op jit(solution)/shard_map/all_gather | solution.py:26
  25.4 393.9 %reduce-scatter.3.cloned.1.call-start = ((), (), s32[]{:S(2)}) async-start(), calls=%async_computation.4 | async-start | bytes 8912896 | tf_op jit(solution)/shard_map/reduce_scatter | solution.py:81
  124.0 142.5 %copy-start.1 = (s32[512]{0:T(512)S(1)}, s32[512]{0:T(512)}, u32[]{:S(2)}) copy-start(s32[512]{0:T(512)} %param.13) | copy-start | bytes 6148
  330.9 88.4 %copy-start.2 = (bf16[256]{0:T(256)(128)(2,1)S(1)}, bf16[256]{0:T(256)(128)(2,1)}, u32[]{:S(2)}) copy-start(bf16[256]{0:T(256)(128)(2,1)} %param.11) | copy-start | bytes 1540
  339.0 111.1 %reduce-scatter.5.cloned.1.call-start = ((), (), s32[]{:S(2)}) async-start(), calls=%async_computation.5 | async-start | bytes 589824 | tf_op jit(solution)/shard_map/reduce_scatter | solution.py:89
  419.9 30.2 %copy-start = (bf16[64,256]{1,0:T(8,128)(2,1)S(1)}, bf16[64,256]{1,0:T(8,128)(2,1)}, u32[]{:S(2)}) copy-start(bf16[64,256]{1,0:T(8,128)(2,1)} %param.10) | copy-start | bytes 98308
Sparse Core Ops, SparseCore 0:
  23.2 58.7 all-gather.5
  85.3 101.5 all-gather.3
  339.1 80.0 reduce-scatter.2
  421.5 28.5 reduce-scatter.4
where the time goes:
time: 516 us
  blocking collectives  289 us (56%)
  waiting for transfers between devices  166 us (32%)
  matrix products  36.1 us (7%)
  between operations  13.8 us (3%)
  other arithmetic  8.61 us (2%)
    reduce_scatter x1, waiting for transfers between devices, local(): lax.psum_scatter(lax.dot_general(head_rows, logit_grad, (((1,), (1,)), ((...  80.2 us
    psum x1, blocking collectives, local(): lax.psum(jnp.sum(teacher_wide * teacher_wide, axis=1), ('phase', 'tp'))  68.6 us
    pmax x1, blocking collectives, local(): lax.pmax((jnp.max(teacher_logits, axis=1), jnp.max(student_logits, axis=1...  64.6 us
    psum x1, blocking collectives, local(): lax.psum((jnp.sum(teacher_exp, axis=1), jnp.sum(teacher_exp * (teacher_lo...  63.9 us
    all_gather x1, waiting for transfers between devices, local(): lax.all_gather(teacher_scaled, ('phase', 'tp'), axis=1, tiled=True)  63 us
    psum x1, blocking collectives, local(): lax.psum(jnp.sum(gain_wide * normed_grad * student_wide, axis=1), 'tp')  33.5 us
    reduce_scatter x1, waiting for transfers between devices, local(): lax.psum_scatter(width_part, 'phase', scatter_dimension=1, tiled=True)  23 us
    psum x1, blocking collectives, local(): lax.psum(jnp.sum(normed_grad * student_wide * student_scale[:, None], axi...  22.8 us
  transfers between devices with their start and end apart: 4, of which 3 were waited for; matrix products, arithmetic and copies ran while one was open for 4% of the time, Pallas kernels for 0%

commit v1 on v0

v1 whole, which is shorter than its diff:
```python
import jax
import jax.numpy as jnp
from jax import lax
from jax.experimental import pallas as pl
from jax.experimental.pallas import tpu as pltpu
from jax.sharding import PartitionSpec as P

NORM_EPSILON = 1e-05
LABEL_WEIGHT = 0.5
F32 = jnp.float32
BF16 = jnp.bfloat16
MESH = pl.DeviceIdType.MESH

DT, DS, TOKENS, LOCAL_V = 16384, 4096, 512, 512
SLAB = 64
PART = ((0, 208), (208, 208), (416, 224))
PART_S = ((0, 48), (208, 48), (416, 32))
PART_T = ((48, 160), (256, 160), (448, 192))
TOKEN_T = (0, 160, 320)
ORDER = (("x", "y", "z"), ("y", "z", "x"), ("z", "x", "y"))
RS_PART = ((0, 48), (48, 48), (96, 32))
ALL = slice(None)
LOW, HIGH = pl.ds(0, 2), pl.ds(2, 2)


def comm_kernel(
    t_rows, t_gain, wt_hbm, s_rows, s_gain, ws_hbm, labels,
    loss_out, rows_out, gain_out, xs_out, g_out,
    G, wt, ws, xs, acc_t, sl, base, st, col, scale_s, gains, g_ref, gp, own,
    sib_in, rs_a0, rs_a1, rs_a2, rs_b, rs_c, rs_d, fin, ex_tp0, ex_ph0, ex_tp1, ex_ph1, ex_gain,
    w_sem, out_sem, gain_s, gain_r, s1, r1, s2, r2, s3s, r3s, s3t, r3t, sibs_s, sibs_r, sibt_s, sibt_r,
    ex_s, ex_r, rs_sib_s, rs_sib_r, rs_s, rs_r,
):
    ph = lax.axis_index("phase")
    tp = lax.axis_index("tp")
    c = ph % 2
    me = {"x": ph // 2, "y": tp % 4, "z": tp // 4}
    sib = (ph + 1 - 2 * c, tp)

    def near(axis, step):
        at = dict(me)
        at[axis] = (me[axis] + step + 4) % 4
        return (at["x"] * 2 + c, at["z"] * 4 + at["y"])

    def rel(axis, step):
        return (me[axis] + step + 4) % 4

    def gat(core, at, rows):
        return G.at[core, at["x"], at["z"], at["y"], pl.ds(*rows), :]

    def remote(src, dst, ssem, rsem, to):
        return pltpu.make_async_remote_copy(
            src_ref=src, dst_ref=dst, send_sem=ssem, recv_sem=rsem, device_id=to, device_id_type=MESH
        )

    wt_loads = [pltpu.make_async_copy(wt_hbm.at[i], wt.at[i], w_sem.at[i]) for i in range(4)]
    ws_load = pltpu.make_async_copy(ws_hbm, ws, w_sem.at[4])
    for load in wt_loads:
        load.start()
    ws_load.start()

    barrier = pltpu.get_barrier_semaphore()

    def greet_tp(d, _):
        pl.semaphore_signal(barrier, inc=1, device_id=(ph, (tp + d) % 16), device_id_type=MESH)
        return 0

    def greet_ph(d, _):
        pl.semaphore_signal(barrier, inc=1, device_id=((ph + d) % 8, tp), device_id_type=MESH)
        return 0

    lax.fori_loop(1, 16, greet_tp, 0)
    lax.fori_loop(1, 8, greet_ph, 0)

    mine = G.at[c, me["x"], me["z"], me["y"]]
    wide = t_rows[...].astype(F32)
    scaled = (wide * t_gain[...].astype(F32)).astype(BF16)
    for (row, size), token in zip(PART_T, TOKEN_T):
        mine[pl.ds(row, size), :] = scaled[token : token + size]
    srow = s_rows[...]
    mine[0:48, :] = srow[0:48, 0:128]
    mine[208:224, :] = srow[48:64, 0:128]
    mine[224:256, :] = srow[0:32, 128:256]
    mine[416:448, :] = srow[32:64, 128:256]
    gains[tp] = s_gain[...]
    acc_t[...] = jnp.zeros_like(acc_t)

    pl.semaphore_wait(barrier, 22)

    def p1(p, i):
        axis = ORDER[p][0]
        block = gat(c, me, PART[p])
        return remote(block, block, s1.at[p, i], r1.at[p, i], near(axis, (1, -1, 2)[i]))

    for i in range(3):
        for p in range(3):
            p1(p, i).start()

    def gain_copy(d):
        return remote(gains.at[tp], gains.at[tp], gain_s.at[d], gain_r.at[d], (ph, (tp + d) % 16))

    def gain_start(d, _):
        gain_copy(d).start()
        return 0

    lax.fori_loop(1, 16, gain_start, 0)

    st[...] = jnp.broadcast_to(jnp.sum(wide * wide, axis=1, keepdims=True), st.shape)

    def line(p, two, three, rows, core=None, half=ALL):
        one, second, third = ORDER[p]
        return gat(c if core is None else core, {one: half, second: two, third: three}, rows)

    def p2(p, i):
        axis, third = ORDER[p][1], me[ORDER[p][2]]
        where = (me[axis], me[axis], rel(axis, -1), rel(axis, 1))[i]
        block = line(p, where, third, PART[p], half=(ALL, ALL, LOW, HIGH)[i])
        return remote(block, block, s2.at[p, i], r2.at[p, i], near(axis, (1, -1, 1, -1)[i]))

    def p2_in(p, i):
        axis, third = ORDER[p][1], me[ORDER[p][2]]
        where = (rel(axis, -1), rel(axis, 1), rel(axis, 2), rel(axis, 2))[i]
        block = line(p, where, third, PART[p], half=(ALL, ALL, LOW, HIGH)[i])
        return remote(block, block, s2.at[p, i], r2.at[p, i], near(axis, (1, -1, 1, -1)[i]))

    def plane(p, three, half):
        one, second, third = ORDER[p]
        return gat(c, {one: half, second: ALL, third: three}, PART_S[p])

    def p3s(p, i, receive=False):
        axis = ORDER[p][2]
        if receive:
            where = (rel(axis, -1), rel(axis, 1), rel(axis, 2), rel(axis, 2))[i]
        else:
            where = (me[axis], me[axis], rel(axis, -1), rel(axis, 1))[i]
        block = plane(p, where, (ALL, ALL, LOW, HIGH)[i])
        return remote(block, block, s3s.at[p, i], r3s.at[p, i], near(axis, (1, -1, 1, -1)[i]))

    STEP2 = (0, -1, 1, 2)

    def p3t(p, j, i, receive=False):
        axis = ORDER[p][2]
        if receive:
            where = (rel(axis, -1), rel(axis, 1), rel(axis, 2), rel(axis, 2))[i]
        else:
            where = (me[axis], me[axis], rel(axis, -1), rel(axis, 1))[i]
        block = line(p, rel(ORDER[p][1], STEP2[j]), where, PART_T[p], half=(ALL, ALL, LOW, HIGH)[i])
        return remote(block, block, s3t.at[p, 4 * j + i], r3t.at[p, 4 * j + i], near(axis, (1, -1, 1, -1)[i]))

    def sib_t(p, j, k, receive=False):
        block = line(
            p, rel(ORDER[p][1], STEP2[j]), rel(ORDER[p][2], STEP2[k]), PART_T[p], core=1 - c if receive else c
        )
        return remote(block, block, sibt_s.at[p, 4 * j + k], sibt_r.at[p, 4 * j + k], sib)

    def sib_s(p, receive=False):
        block = G.at[1 - c if receive else c, :, :, :, pl.ds(*PART_S[p]), :]
        return remote(block, block, sibs_s.at[p], sibs_r.at[p], sib)

    def p3t_send(j):
        for p in range(3):
            p3t(p, j, 0).start()
            p3t(p, j, 1).start()

    def consume(j, k):
        for p in range(3):
            sib_t(p, j, k, receive=True).wait_recv()

        def one_core(core, _):
            for p in range(3):
                one, second, third = ORDER[p]
                at = {one: ALL, second: rel(second, STEP2[j]), third: rel(third, STEP2[k])}
                rows = G[core, at["x"], at["z"], at["y"], pl.ds(*PART_T[p]), :]
                lhs = jnp.concatenate([rows[i] for i in range(4)], axis=1)
                rhs = wt[at["x"], core, at["z"], at["y"]].reshape(512, LOCAL_V)
                acc_t[pl.ds(TOKEN_T[p], PART_T[p][1]), :] += jnp.dot(lhs, rhs, preferred_element_type=F32)
            return 0

        lax.fori_loop(0, 2, one_core, 0)

    for p in range(3):
        for i in range(3):
            p1(p, i).wait_recv()
        p2(p, 0).start()
        p2(p, 1).start()
    p3t_send(0)
    for i in (0, 1):
        for p in range(3):
            p2_in(p, i).wait_recv()
            p2(p, i + 2).start()
    for p in range(3):
        sib_t(p, 0, 0).start()
    for p in range(3):
        p2_in(p, 2).wait_recv()
        p2_in(p, 3).wait_recv()
        p3s(p, 0).start()
        p3s(p, 1).start()
    p3t_send(1)
    for load in wt_loads:
        load.wait()
    ws_load.wait()
    consume(0, 0)
    for j in (1, 2, 3):
        for p in range(3):
            sib_t(p, j, 0).start()
    for i in (0, 1):
        for p in range(3):
            p3s(p, i, True).wait_recv()
            p3s(p, i + 2).start()
    consume(1, 0)

    def forward(j):
        for i in (0, 1):
            for p in range(3):
                p3t(p, j, i, True).wait_recv()
                p3t(p, j, i + 2).start()
                sib_t(p, j, i + 1).start()

    def opposite(j):
        for p in range(3):
            p3t(p, j, 2, True).wait_recv()
            p3t(p, j, 3, True).wait_recv()
            sib_t(p, j, 3).start()

    forward(0)
    for p in range(3):
        p3s(p, 2, True).wait_recv()
        p3s(p, 3, True).wait_recv()
        sib_s(p).start()
    p3t_send(2)
    consume(0, 1)
    consume(0, 2)
    opposite(0)
    p3t_send(3)

    def gain_wait(d, _):
        gain_copy(d).wait()
        return 0

    lax.fori_loop(1, 16, gain_wait, 0)
    for p in range(3):
        sib_s(p, True).wait_recv()

    def halves(q, t):
        block = G.at[q % 2, q // 2, t // 4, t % 4]
        first = jnp.concatenate([block[0:48, :], block[208:224, :]], axis=0)
        second = jnp.concatenate([block[224:256, :], block[416:448, :]], axis=0)
        return first.astype(F32), second.astype(F32)

    def norm_slab(q, _):
        def squares(t, total):
            first, second = halves(q, t)
            return total + first * first + second * second

        total = lax.fori_loop(0, 16, squares, jnp.zeros((SLAB, 128), F32))
        scale = lax.rsqrt(jnp.sum(total, axis=1, keepdims=True) / DS + NORM_EPSILON)
        rows = pl.ds(pl.multiple_of(q * SLAB, SLAB), SLAB)
        scale_s[rows, :] = scale

        def normed(t, _):
            first, second = halves(q, t)
            gain = gains[t].astype(F32)
            xs[t, rows, 0:128] = (first * scale * gain[0:1, :]).astype(BF16)
            xs[t, rows, 128:256] = (second * scale * gain[1:2, :]).astype(BF16)
            return 0

        lax.fori_loop(0, 16, normed, 0)
        return 0

    lax.fori_loop(0, 8, norm_slab, 0)
    xs_copy = pltpu.make_async_copy(xs, xs_out, out_sem.at[0])
    xs_copy.start()
    forward(1)

    sl[...] = jnp.dot(xs[0], ws[0], preferred_element_type=F32)

    def student_dot(t, _):
        sl[...] += jnp.dot(xs[t], ws[t], preferred_element_type=F32)
        return 0

    lax.fori_loop(1, 16, student_dot, 0)
    vocab_first = (ph * 16 + tp) * LOCAL_V
    lane = lax.broadcasted_iota(jnp.int32, (SLAB, 128), 1)

    def slab(q):
        return pl.ds(pl.multiple_of(q * SLAB, SLAB), SLAB)

    def label_hit(rows):
        ids = vocab_first + lax.broadcasted_iota(jnp.int32, (SLAB, LOCAL_V), 1)
        return labels[rows, :] == ids

    def pack(columns):
        out = jnp.zeros((SLAB, 128), F32)
        for i, column in enumerate(columns):
            out = jnp.where(lane == i, column, out)
        return out

    def rowsum(value):
        return jnp.sum(value, axis=1, keepdims=True)

    def student_stats(q, _):
        rows = slab(q)
        logits = sl[rows, :]
        top = jnp.max(logits, axis=1, keepdims=True)
        e = jnp.exp(logits - top)
        picked = jnp.where(label_hit(rows), logits, 0.0)
        st[rows, :] = pack([top, rowsum(e), rowsum(e * logits), rowsum(picked), st[rows, 0:1]])
        return 0

    lax.fori_loop(0, 8, student_stats, 0)

    def exchange_start(buf, own_slot, count, number, to):
        def start(d, _):
            remote(buf.at[own_slot], buf.at[own_slot], ex_s.at[number, d], ex_r.at[number, d], to(d)).start()
            return 0

        lax.fori_loop(1, count, start, 0)

    def exchange_wait(buf, own_slot, count, number, to):
        def wait(d, _):
            remote(buf.at[own_slot], buf.at[own_slot], ex_s.at[number, d], ex_r.at[number, d], to(d)).wait()
            return 0

        lax.fori_loop(1, count, wait, 0)

    def to_tp(d):
        return (ph, (tp + d) % 16)

    def to_ph(d):
        return ((ph + d) % 8, tp)

    sub = lax.broadcasted_iota(jnp.int32, (8, TOKENS), 0)

    def merge(buf, count, weighted):
        top = buf[0][0:1, :]
        for i in range(1, count):
            top = jnp.maximum(top, buf[i][0:1, :])
        total = jnp.zeros((8, TOKENS), F32)
        for i in range(count):
            part = buf[i]
            weight = jnp.exp(part[0:1, :] - top)
            total = total + part * jnp.where(sub <= weighted, weight, 1.0)
        return jnp.where(sub == 0, top, total)

    def transposed_stats():
        return jnp.transpose(st[...])[0:8, :]

    ex_tp0[tp] = transposed_stats()
    exchange_start(ex_tp0, tp, 16, 0, to_tp)
    opposite(1)
    consume(0, 3)
    consume(1, 1)
    consume(1, 2)
    exchange_wait(ex_tp0, tp, 16, 0, to_tp)
    ex_ph0[ph] = merge(ex_tp0, 16, 2)
    exchange_start(ex_ph0, ph, 8, 1, to_ph)
    forward(2)
    consume(2, 0)
    consume(1, 3)
    consume(2, 1)
    consume(2, 2)
    exchange_wait(ex_ph0, ph, 8, 1, to_ph)
    early = merge(ex_ph0, 8, 2)
    student_top, student_total, student_inner = early[0:1], early[1:2], early[2:3] / early[1:2]
    picked_all, squares_all = early[3:4], early[4:5]
    student_lse = student_top + jnp.log(student_total)
    teacher_scale = lax.rsqrt(squares_all / DT + NORM_EPSILON)

    def to_columns(rows):
        block = jnp.concatenate(rows + [jnp.zeros((128 - len(rows), TOKENS), F32)], axis=0)
        return jnp.transpose(block)

    col[...] = to_columns([student_lse, teacher_scale])

    def student_grad(q, _):
        rows = slab(q)
        prob = jnp.exp(sl[rows, :] - col[rows, 0:1])
        base[rows, :] = (1.0 + LABEL_WEIGHT) * prob - LABEL_WEIGHT * label_hit(rows).astype(F32)
        return 0

    lax.fori_loop(0, 8, student_grad, 0)
    forward(3)
    opposite(2)
    consume(3, 0)
    consume(3, 1)
    consume(3, 2)
    consume(2, 3)
    opposite(3)
    consume(3, 3)

    def teacher_stats(q, _):
        rows = slab(q)
        logits = acc_t[rows, :] * col[rows, 1:2]
        student = sl[rows, :]
        top = jnp.max(logits, axis=1, keepdims=True)
        e = jnp.exp(logits - top)
        acc_t[rows, :] = e
        st[rows, :] = pack([top, rowsum(e), rowsum(e * (logits - student)), rowsum(e * student)])
        return 0

    lax.fori_loop(0, 8, teacher_stats, 0)
    local_stats = transposed_stats()
    ex_tp1[tp] = local_stats
    exchange_start(ex_tp1, tp, 16, 2, to_tp)
    exchange_wait(ex_tp1, tp, 16, 2, to_tp)
    ex_ph1[ph] = merge(ex_tp1, 16, 3)
    exchange_start(ex_ph1, ph, 8, 3, to_ph)
    exchange_wait(ex_ph1, ph, 8, 3, to_ph)
    late = merge(ex_ph1, 8, 3)
    teacher_top, teacher_total = late[0:1], late[1:2]
    teacher_lse = teacher_top + jnp.log(teacher_total)
    loss = (
        late[2:3] / teacher_total - teacher_lse + student_lse + LABEL_WEIGHT * (student_lse - picked_all)
    )
    inner = (1.0 + LABEL_WEIGHT) * student_inner - late[3:4] / teacher_total - LABEL_WEIGHT * picked_all
    factor = jnp.exp(local_stats[0:1] - teacher_top) / teacher_total
    col[...] = to_columns([factor, inner, loss])

    def logit_grad(q, _):
        rows = slab(q)
        g = (base[rows, :] - acc_t[rows, :] * col[rows, 0:1]).astype(BF16)
        g_ref[rows, :] = g
        gp[(q + c) % 2, pl.ds(pl.multiple_of((q // 2) * SLAB, SLAB), SLAB), :] = g
        return 0

    lax.fori_loop(0, 8, logit_grad, 0)
    g_copy = pltpu.make_async_copy(g_ref, g_out, out_sem.at[1])
    g_copy.start()

    def sib_chunks(t):
        return wt.at[:, 0, t // 4, t % 4, :, pl.ds(0, 128)]

    def rs_sib(t):
        return remote(sib_chunks(t), sib_in.at[:, t // 4, t % 4], rs_sib_s.at[t], rs_sib_r.at[t], sib)

    def nt_dot(lhs, rhs):
        return lax.dot_general(lhs, rhs, (((1,), (1,)), ((), ())), preferred_element_type=F32)

    def sib_part(t, _):
        r = nt_dot(gp[1], ws[t]).astype(BF16)
        for xt in range(4):
            wt[xt, 0, t // 4, t % 4, 0:64, 0:128] = r[xt * 64 : xt * 64 + 64, 0:128]
            wt[xt, 0, t // 4, t % 4, 64:128, 0:128] = r[xt * 64 : xt * 64 + 64, 128:256]
        rs_sib(t).start()
        return 0

    lax.fori_loop(0, 16, sib_part, 0)

    def own_part(t, _):
        r = nt_dot(gp[0], ws[t])
        rs_sib(t).wait_recv()
        for xt in range(4):
            other = sib_in[xt, t // 4, t % 4].astype(F32)
            own[xt, t // 4, t % 4, 0:64] = r[xt * 64 : xt * 64 + 64, 0:128] + other[0:64]
            own[xt, t // 4, t % 4, 64:128] = r[xt * 64 : xt * 64 + 64, 128:256] + other[64:128]
        return 0

    lax.fori_loop(0, 16, own_part, 0)

    def at3(p, one, two, three):
        a, b, d = ORDER[p]
        at = {a: one, b: two, d: three}
        return at["x"], at["z"], at["y"]

    def stage_ref(p, one, two, three):
        ix, iz, iy = at3(p, one, two, three)
        return wt.at[ix, 0, iz, iy, pl.ds(*RS_PART[p]), pl.ds(128, 128)]

    def own_ref(p, one, two, three):
        ix, iz, iy = at3(p, one, two, three)
        return own.at[ix, iz, iy, pl.ds(*RS_PART[p]), :]

    def rest(p, two, three):
        at = {ORDER[p][1]: two, ORDER[p][2]: three}
        return tuple(at[k] for k in ("x", "z", "y") if k in at)

    rs_a = (rs_a0, rs_a1, rs_a2)

    def stage(p, one, two, three):
        stage_ref(p, one, two, three)[...] = own_ref(p, one, two, three)[...].astype(BF16)

    def rs_copy(src, dst, p, i, to):
        return remote(src, dst, rs_s.at[p, i], rs_r.at[p, i], to)

    def rs1(p, i):
        axis = ORDER[p][0]
        src = stage_ref(p, rel(axis, 2), (LOW, HIGH)[i], ALL)
        return rs_copy(src, rs_a[p].at[i], p, i, near(axis, (1, -1)[i]))

    def rs2(p, i):
        axis = ORDER[p][0]
        src = stage_ref(p, rel(axis, (1, -1)[i]), ALL, ALL)
        return rs_copy(src, rs_b.at[i, :, :, pl.ds(*RS_PART[p]), :], p, 2 + i, near(axis, (1, -1)[i]))

    def rs3(p, i):
        axis = ORDER[p][1]
        src = stage_ref(p, me[ORDER[p][0]], rel(axis, (1, -1, 2)[i]), ALL)
        return rs_copy(src, rs_c.at[i, :, pl.ds(*RS_PART[p]), :], p, 4 + i, near(axis, (1, -1, 2)[i]))

    def rs4(p, i):
        axis = ORDER[p][2]
        src = stage_ref(p, me[ORDER[p][0]], me[ORDER[p][1]], rel(axis, (1, -1, 2)[i]))
        return rs_copy(src, rs_d.at[i, pl.ds(*RS_PART[p]), :], p, 7 + i, near(axis, (1, -1, 2)[i]))

    for p in range(3):
        def far(n, _, p=p):
            stage(p, rel(ORDER[p][0], 2), n // 4, n % 4)
            return 0

        lax.fori_loop(0, 16, far, 0)
        rs1(p, 0).start()
        rs1(p, 1).start()
    for p in range(3):
        rows = pl.ds(*RS_PART[p])
        for i in range(2):
            rs1(p, i).wait_recv()

            def pass_on(n, _, p=p, i=i, rows=rows):
                target = rel(ORDER[p][0], (1, -1)[i])
                near_half = n // 4
                two = near_half + 2 * i
                stage_ref(p, target, two, n % 4)[...] = (
                    own_ref(p, target, two, n % 4)[...] + rs_a[p][(i, *rest(p, near_half, n % 4))].astype(F32)
                ).astype(BF16)
                stage(p, target, near_half + 2 * (1 - i), n % 4)
                return 0

            lax.fori_loop(0, 8, pass_on, 0)
            rs2(p, i).start()
    for p in range(3):
        rows = pl.ds(*RS_PART[p])
        rs2(p, 0).wait_recv()
        rs2(p, 1).wait_recv()

        def add_first(n, _, p=p, rows=rows):
            ref = own_ref(p, me[ORDER[p][0]], n // 4, n % 4)
            total = (
                ref[...]
                + rs_b[(0, *rest(p, n // 4, n % 4), rows, ALL)].astype(F32)
                + rs_b[(1, *rest(p, n // 4, n % 4), rows, ALL)].astype(F32)
            )
            ref[...] = total
            stage_ref(p, me[ORDER[p][0]], n // 4, n % 4)[...] = total.astype(BF16)
            return 0

        lax.fori_loop(0, 16, add_first, 0)
        for i in (2, 0, 1):
            rs3(p, i).start()
    for p in range(3):
        rows = pl.ds(*RS_PART[p])
        for i in range(3):
            rs3(p, i).wait_recv()

        def add_second(n, _, p=p, rows=rows):
            ref = own_ref(p, me[ORDER[p][0]], me[ORDER[p][1]], n)
            total = ref[...]
            for i in range(3):
                total = total + rs_c[i, n, rows, :].astype(F32)
            ref[...] = total
            stage_ref(p, me[ORDER[p][0]], me[ORDER[p][1]], n)[...] = total.astype(BF16)
            return 0

        lax.fori_loop(0, 4, add_second, 0)
        for i in (2, 0, 1):
            rs4(p, i).start()
    for p in range(3):
        rows = pl.ds(*RS_PART[p])
        for i in range(3):
            rs4(p, i).wait_recv()
        total = own_ref(p, me[ORDER[p][0]], me[ORDER[p][1]], me[ORDER[p][2]])[...]
        for i in range(3):
            total = total + rs_d[i, rows, :].astype(F32)
        fin[rows, :] = total

    rows = slab(ph)
    scale = scale_s[rows, :]
    inner_own = col[rows, 1:2]
    raw = s_rows[...].astype(F32)
    gain = s_gain[...].astype(F32)
    coefficient = scale * scale * inner_own / DS
    parts = []
    for h in range(2):
        grad = fin[h * 64 : h * 64 + 64, :]
        wide_h = raw[:, h * 128 : h * 128 + 128]
        rows_out[:, h * 128 : h * 128 + 128] = (scale * gain[h : h + 1] * grad - wide_h * coefficient).astype(BF16)
        parts.append(jnp.sum(grad * wide_h * scale, axis=0, keepdims=True))
    ex_gain[ph] = jnp.broadcast_to(jnp.concatenate(parts, axis=1), (8, 256))
    exchange_start(ex_gain, ph, 8, 4, to_ph)
    base[0:8, :] = jnp.broadcast_to(loss, (8, TOKENS))
    window = base[0:1, pl.ds(pl.multiple_of(me["x"] * 128, 128), 128)]
    loss_out[...] = jnp.where(c == 1, window[:, 64:128], window[:, 0:64])
    exchange_wait(ex_gain, ph, 8, 4, to_ph)
    total = ex_gain[0]
    for i in range(1, 8):
        total = total + ex_gain[i]
    gain_out[...] = total[0:1]

    for p in range(3):
        for i in range(3):
            p1(p, i).wait_send()
        for i in range(4):
            p2(p, i).wait_send()
            p3s(p, i).wait_send()
        sib_s(p).wait_send()
        for j in range(4):
            for i in range(4):
                p3t(p, j, i).wait_send()
                sib_t(p, j, i).wait_send()
        for i in range(2):
            rs1(p, i).wait_send()
            rs2(p, i).wait_send()
        for i in range(3):
            rs3(p, i).wait_send()
            rs4(p, i).wait_send()

    def sib_sent(t, _):
        rs_sib(t).wait_send()
        return 0

    lax.fori_loop(0, 16, sib_sent, 0)
    xs_copy.wait()
    g_copy.wait()


def head_kernel(xs_ref, g_ref, out_ref):
    out_ref[...] = lax.dot_general(
        xs_ref[0], g_ref[...], (((0,), (0,)), ((), ())), preferred_element_type=F32
    ).astype(BF16)


def local(teacher_rows, teacher_gain, teacher_head, student_rows, student_gain, student_head, labels):
    vmem = pl.BlockSpec(memory_space=pltpu.VMEM)
    hbm = pl.BlockSpec(memory_space=pl.ANY)
    dma = pltpu.SemaphoreType.DMA
    loss, rows_grad, gain_grad, xs, g = pl.pallas_call(
        comm_kernel,
        out_shape=(
            jax.ShapeDtypeStruct((1, SLAB), F32),
            jax.ShapeDtypeStruct((SLAB, 256), BF16),
            jax.ShapeDtypeStruct((1, 256), F32),
            jax.ShapeDtypeStruct((16, TOKENS, 256), BF16),
            jax.ShapeDtypeStruct((TOKENS, LOCAL_V), BF16),
        ),
        in_specs=[vmem, vmem, hbm, vmem, vmem, hbm, vmem],
        out_specs=(vmem, vmem, vmem, hbm, hbm),
        scratch_shapes=[
            pltpu.VMEM((2, 4, 4, 4, 640, 128), BF16),
            pltpu.VMEM((4, 2, 4, 4, 128, LOCAL_V), BF16),
            pltpu.VMEM((16, 256, LOCAL_V), BF16),
            pltpu.VMEM((16, TOKENS, 256), BF16),
            pltpu.VMEM((TOKENS, LOCAL_V), F32),
            pltpu.VMEM((TOKENS, LOCAL_V), F32),
            pltpu.VMEM((TOKENS, LOCAL_V), F32),
            pltpu.VMEM((TOKENS, 128), F32),
            pltpu.VMEM((TOKENS, 128), F32),
            pltpu.VMEM((TOKENS, 1), F32),
            pltpu.VMEM((16, 2, 128), BF16),
            pltpu.VMEM((TOKENS, LOCAL_V), BF16),
            pltpu.VMEM((2, 256, LOCAL_V), BF16),
            pltpu.VMEM((4, 4, 4, 128, 128), F32),
            pltpu.VMEM((4, 4, 4, 128, 128), BF16),
            pltpu.VMEM((2, 4, 2, 48, 128), BF16),
            pltpu.VMEM((2, 4, 2, 48, 128), BF16),
            pltpu.VMEM((2, 2, 4, 32, 128), BF16),
            pltpu.VMEM((2, 4, 4, 128, 128), BF16),
            pltpu.VMEM((3, 4, 128, 128), BF16),
            pltpu.VMEM((3, 128, 128), BF16),
            pltpu.VMEM((128, 128), F32),
            pltpu.VMEM((16, 8, TOKENS), F32),
            pltpu.VMEM((8, 8, TOKENS), F32),
            pltpu.VMEM((16, 8, TOKENS), F32),
            pltpu.VMEM((8, 8, TOKENS), F32),
            pltpu.VMEM((8, 8, 256), F32),
            dma((5,)), dma((2,)), dma((16,)), dma((16,)),
            dma((3, 3)), dma((3, 3)), dma((3, 4)), dma((3, 4)), dma((3, 4)), dma((3, 4)),
            dma((3, 16)), dma((3, 16)), dma((3,)), dma((3,)), dma((3, 16)), dma((3, 16)),
            dma((5, 16)), dma((5, 16)), dma((16,)), dma((16,)), dma((3, 10)), dma((3, 10)),
        ],
        compiler_params=pltpu.CompilerParams(
            collective_id=0, has_side_effects=True, vmem_limit_bytes=63 << 20
        ),
        name="distill",
    )(
        teacher_rows,
        teacher_gain.reshape(1, 128),
        teacher_head.reshape(4, 2, 4, 4, 128, LOCAL_V),
        student_rows,
        student_gain.reshape(2, 128),
        student_head.reshape(16, 256, LOCAL_V),
        labels.reshape(TOKENS, 1),
    )
    head_grad = pl.pallas_call(
        head_kernel,
        grid=(16,),
        out_shape=jax.ShapeDtypeStruct((DS, LOCAL_V), BF16),
        in_specs=[
            pl.BlockSpec((1, TOKENS, 256), lambda t: (t, 0, 0)),
            pl.BlockSpec((TOKENS, LOCAL_V), lambda t: (0, 0)),
        ],
        out_specs=pl.BlockSpec((256, LOCAL_V), lambda t: (t, 0)),
        name="head_grad",
    )(xs, g)
    return loss.reshape(SLAB), head_grad, rows_grad, gain_grad.reshape(256)


def solution(mesh):
    placed = (
        P(None, ("phase", "tp")),
        P(("phase", "tp")),
        P(None, ("phase", "tp")),
        P("phase", "tp"),
        P("tp"),
        P(None, ("phase", "tp")),
        P(),
    )
    return jax.shard_map(
        local,
        mesh=mesh,
        in_specs=placed,
        out_specs=(P("phase"), P(None, ("phase", "tp")), P("phase", "tp"), P("tp")),
        check_vma=False,
    )
```

time: 516 us -> 142 us (0.28)
  blocking collectives: 289 us -> 0 us
  waiting for transfers between devices: 166 us -> 0 us
  Pallas kernels: 0 us -> 138 us
  matrix products: 36.1 us -> 0 us
  between operations: 13.8 us -> 0.67 us
  other arithmetic: 8.61 us -> 0 us
    psum x4 -> x0, blocking collectives: 189 us -> none  [the longest x1 68.6 us: local(): lax.psum(jnp.sum(teacher_wide * teacher_wide, axis=1), ('phase', 'tp'))]
    pallas_call x0 -> x2, Pallas kernels: none -> 138 us  [the longest x1 125 us: local(): pl.pallas_call(comm_kernel, out_shape=(jax.ShapeDtypeStruct((1, SLAB), F3...]
    reduce_scatter x2 -> x0, waiting for transfers between devices: 103 us -> none  [the longest x1 80.2 us: local(): lax.psum_scatter(lax.dot_general(head_rows, logit_grad, (((1,), (1,)), ((...]
    pmax x1 -> x0, blocking collectives: 64.6 us -> none  [local(): lax.pmax((jnp.max(teacher_logits, axis=1), jnp.max(student_logits, axis=1...]
    all_gather x2 -> x0, waiting for transfers between devices: 63 us -> none  [the longest x1 63 us: local(): lax.all_gather(teacher_scaled, ('phase', 'tp'), axis=1, tiled=True)]
    dot_general x4 -> x0, matrix products: 36.1 us -> none  [the longest x1 14.9 us: local(): jnp.dot(lax.all_gather(teacher_scaled, ('phase', 'tp'), axis=1, tiled=Tru...]
    all_gather x2 -> x0, blocking collectives: 35.9 us -> none  [the longest x1 20.1 us: local(): lax.all_gather(student_gain, 'tp', axis=0, tiled=True)]
    reduce_sum x4 -> x0, other arithmetic: 6.27 us -> none  [the longest x1 3.13 us: local(): jnp.mean(full_wide * full_wide, axis=1) + NORM_EPSILON]
  transfers between devices with their start and end apart: 4 -> 0, of which waited for: 3 -> 0; matrix products, arithmetic and copies ran while one was open for 4% -> 0% of each run, Pallas kernels for 0% -> 0%
where the time goes in v1:
time: 142 us
  Pallas kernels  138 us (97%)
  local copies, waits for them, and re-layouts  3.24 us (2%)
    pallas_call x1, Pallas kernels, local(): pl.pallas_call(comm_kernel, out_shape=(jax.ShapeDtypeStruct((1, SLAB), F3...  125 us
    pallas_call x1, Pallas kernels, local(): pl.pallas_call(head_kernel, grid=(16,), out_shape=jax.ShapeDtypeStruct((D...  12.6 us

profile of v1, /device:TPU:1, one launch (start us, length us, event | category | flops | bytes accessed | tf_op | source)
XLA Modules:
  0.0 141.8 jit_solution(17639355746326578272)
XLA Ops:
  0.6 1.5 %copy.11.labels = s32[512,1]{1,0:T(8,128)} copy(s32[512,1]{0,1:T(1,128)} %bitcast.9) | data formatting | bytes 4096 | tf_op jit(solution)/shard_map/reshape | solution.py:690
  2.2 125.3 %distill.1 = (f32[1,64]{1,0:T(1,128)}, bf16[64,256]{1,0:T(8,128)(2,1)}, f32[1,256]{1,0:T(1,128)}, bf16[16,512,256]{2,1,0:T(8,128)(2,1)}, bf16[512,512]{1,0:T(8,128)(2,1)}) custom-call(bf16[512,128]{1,0:T(8,128)(2,1)} %t_rows.1, bf16[1,128]{1,0:T(2,128)(2,1)} %bitcast.11, bf16[4,2,4,4,128,512]{5,4,3,2,1,0:T(8,128)(2,1)} %bitcast.7, bf16[64,256]{1,0:T(8,128)(2,1)} %s_rows.1, ...), custom_call_target="tpu_custom_call" | custom-call | tf_op jit(solution)/shard_map/distill/pallas_call | solution.py:635
  127.5 0.0 copy-start.2
  127.5 0.0 copy-start
  127.5 0.0 copy-start.1
  127.5 12.6 %head_grad.1 = bf16[4096,512]{1,0:T(8,128)(2,1)} custom-call(bf16[16,512,256]{2,1,0:T(8,128)(2,1)} %get-tuple-element.10.xs_ref, bf16[512,512]{1,0:T(8,128)(2,1)} %get-tuple-element.11.g_ref), custom_call_target="tpu_custom_call" | custom-call | tf_op jit(solution)/shard_map/head_grad/pallas_call | solution.py:692
  140.1 0.0 copy-done.2
  140.1 0.5 copy.15
  140.6 0.0 copy-done
  140.6 0.6 copy.16
  141.2 0.0 copy-done.1
  141.2 0.6 copy.17
Async XLA Ops:
  127.5 12.6 %copy-start.2 = (f32[1,64]{1,0:T(1,128)S(1)}, f32[1,64]{1,0:T(1,128)}, u32[]{:S(2)}) copy-start(f32[1,64]{1,0:T(1,128)} %get-tuple-element.9) | copy-start | bytes 772
  127.5 13.1 %copy-start = (bf16[64,256]{1,0:T(8,128)(2,1)S(1)}, bf16[64,256]{1,0:T(8,128)(2,1)}, u32[]{:S(2)}) copy-start(bf16[64,256]{1,0:T(8,128)(2,1)} %get-tuple-element.20) | copy-start | bytes 98308
  127.5 13.7 %copy-start.1 = (f32[1,256]{1,0:T(1,128)S(1)}, f32[1,256]{1,0:T(1,128)}, u32[]{:S(2)}) copy-start(f32[1,256]{1,0:T(1,128)} %get-tuple-element.13) | copy-start | bytes 3076

commit v2 on v0

v2 whole, which is shorter than its diff:
```python
import jax
import jax.numpy as jnp
from jax import lax
from jax.experimental import pallas as pl
from jax.experimental.pallas import tpu as pltpu
from jax.sharding import PartitionSpec as P

NORM_EPSILON = 1e-05
LABEL_WEIGHT = 0.5
F32 = jnp.float32
BF16 = jnp.bfloat16
MESH = pl.DeviceIdType.MESH

DT, DS, TOKENS, LOCAL_V = 16384, 4096, 512, 512
SLAB = 64
PART = ((0, 208), (208, 208), (416, 224))
PART_S = ((0, 48), (208, 48), (416, 32))
PART_T = ((48, 160), (256, 160), (448, 192))
TOKEN_T = (0, 160, 320)
ORDER = (("x", "y", "z"), ("y", "z", "x"), ("z", "x", "y"))
RS_PART = ((0, 48), (48, 48), (96, 32))
ALL = slice(None)
LOW, HIGH = pl.ds(0, 2), pl.ds(2, 2)


def comm_kernel(
    t_rows, t_gain, wt_hbm, s_rows, s_gain, ws_hbm, labels,
    loss_out, rows_out, gain_out, xst_out, g_out,
    G, wt, ws, ws_sib, xs, xst, acc_t, sl, es, st, col, lab, scale_s, g_ref, gp, gp_in, own,
    rs_b, rs_c, rs_d, fin, ex_tp0, ex_ph0, ex_tp1, ex_ph1, ex_gain,
    w_sem, out_sem, s1, r1, s2, r2, s2f, r2f, s3s, r3s, s3t, r3t, sibs_s, sibs_r, sibt_s, sibt_r,
    ex_s, ex_r, misc_s, misc_r, rs_s, rs_r,
):
    ph = lax.axis_index("phase")
    tp = lax.axis_index("tp")
    c = ph % 2
    me = {"x": ph // 2, "y": tp % 4, "z": tp // 4}
    sib = (ph + 1 - 2 * c, tp)
    PARTS = range(3)
    STEP = (0, -1, 1, 2)

    def rel(axis, step):
        return (me[axis] + step + 4) % 4

    def near(axis, step):
        at = dict(me)
        at[axis] = rel(axis, step)
        return (at["x"] * 2 + c, at["z"] * 4 + at["y"])

    def remote(src, dst, ssem, rsem, to):
        return pltpu.make_async_remote_copy(
            src_ref=src, dst_ref=dst, send_sem=ssem, recv_sem=rsem, device_id=to, device_id_type=MESH
        )

    wt_loads = [pltpu.make_async_copy(wt_hbm.at[i], wt.at[i], w_sem.at[i]) for i in range(4)]
    ws_load = pltpu.make_async_copy(ws_hbm, ws, w_sem.at[4])
    ws_load.start()
    for load in wt_loads:
        load.start()

    barrier = pltpu.get_barrier_semaphore()
    partners = [sib] + [near(axis, step) for axis in "xyz" for step in (1, -1, 2)]
    for to in partners:
        pl.semaphore_signal(barrier, inc=1, device_id=to, device_id_type=MESH)

    mine = G.at[c, me["x"], me["z"], me["y"]]
    wide = t_rows[...].astype(F32)
    scaled = (wide * t_gain[...].astype(F32)).astype(BF16)
    for (row, size), token in zip(PART_T, TOKEN_T):
        mine[pl.ds(row, size), :] = scaled[token : token + size]
    srow = s_rows[...]
    mine[0:48, :] = srow[0:48, 0:128]
    mine[208:224, :] = srow[48:64, 0:128]
    mine[224:256, :] = srow[0:32, 128:256]
    mine[416:448, :] = srow[32:64, 128:256]

    pl.semaphore_wait(barrier, len(partners))

    def block(p, one, two, three, rows, core=None):
        a, b, d = ORDER[p]
        at = {a: one, b: two, d: three}
        return G.at[c if core is None else core, at["x"], at["z"], at["y"], pl.ds(*rows), :]

    def own_at(p):
        return tuple(me[axis] for axis in ORDER[p])

    def p1(p, i):
        ref = block(p, *own_at(p), PART[p])
        return remote(ref, ref, s1.at[p, i], r1.at[p, i], near(ORDER[p][0], (-1, 1, 2)[i]))

    def p2(p, n, i):
        a, b, d = ORDER[p]
        ref = block(p, rel(a, STEP[n]), me[b], me[d], PART[p])
        return remote(ref, ref, s2.at[p, 2 * n + i], r2.at[p, 2 * n + i], near(b, (1, -1)[i]))

    def p2f(p, i):
        a, b, d = ORDER[p]
        ref = block(p, (LOW, HIGH)[i], rel(b, (-1, 1)[i]), me[d], PART[p])
        return remote(ref, ref, s2f.at[p, i], r2f.at[p, i], near(b, (1, -1)[i]))

    def p3s(p, i):
        d = ORDER[p][2]
        ref = block(p, (ALL, ALL, LOW, HIGH)[i], ALL, rel(d, (0, 0, -1, 1)[i]), PART_S[p])
        return remote(ref, ref, s3s.at[p, i], r3s.at[p, i], near(d, (1, -1, 1, -1)[i]))

    def p3t(p, j, i):
        a, b, d = ORDER[p]
        ref = block(p, (ALL, ALL, LOW, HIGH)[i], rel(b, STEP[j]), rel(d, (0, 0, -1, 1)[i]), PART_T[p])
        return remote(ref, ref, s3t.at[p, 4 * j + i], r3t.at[p, 4 * j + i], near(d, (1, -1, 1, -1)[i]))

    def p2_wait(p, n, i):
        a, b, d = ORDER[p]
        ref = block(p, rel(a, STEP[n]), rel(b, (-1, 1)[i]), me[d], PART[p])
        remote(ref, ref, s2.at[p, 2 * n + i], r2.at[p, 2 * n + i], sib).wait_recv()

    def p2f_wait(p, i):
        a, b, d = ORDER[p]
        ref = block(p, (LOW, HIGH)[i], rel(b, 2), me[d], PART[p])
        remote(ref, ref, s2f.at[p, i], r2f.at[p, i], sib).wait_recv()

    def p3s_wait(p, i):
        d = ORDER[p][2]
        ref = block(p, (ALL, ALL, LOW, HIGH)[i], ALL, rel(d, (-1, 1, 2, 2)[i]), PART_S[p])
        remote(ref, ref, s3s.at[p, i], r3s.at[p, i], sib).wait_recv()

    def p3t_wait(p, j, i):
        a, b, d = ORDER[p]
        ref = block(p, (ALL, ALL, LOW, HIGH)[i], rel(b, STEP[j]), rel(d, (-1, 1, 2, 2)[i]), PART_T[p])
        remote(ref, ref, s3t.at[p, 4 * j + i], r3t.at[p, 4 * j + i], sib).wait_recv()

    def sib_t(p, j, k, core=None):
        a, b, d = ORDER[p]
        ref = block(p, ALL, rel(b, STEP[j]), rel(d, STEP[k]), PART_T[p], core)
        return remote(ref, ref, sibt_s.at[p, 4 * j + k], sibt_r.at[p, 4 * j + k], sib)

    def sib_s(p, core):
        ref = G.at[core, :, :, :, pl.ds(*PART_S[p]), :]
        return remote(ref, ref, sibs_s.at[p], sibs_r.at[p], sib)

    def p3t_send(j):
        for p in PARTS:
            p3t(p, j, 0).start()
            p3t(p, j, 1).start()

    def products(j, k, core):
        for p in PARTS:
            a, b, d = ORDER[p]
            at = {a: ALL, b: rel(b, STEP[j]), d: rel(d, STEP[k])}
            rows = G[core, at["x"], at["z"], at["y"], pl.ds(*PART_T[p]), :]
            lhs = jnp.concatenate([rows[i] for i in range(4)], axis=1)
            rhs = wt[at["x"], core, at["z"], at["y"]].reshape(512, LOCAL_V)
            acc_t[pl.ds(TOKEN_T[p], PART_T[p][1]), :] += jnp.dot(lhs, rhs, preferred_element_type=F32)

    def sib_wait(j, k):
        for p in PARTS:
            sib_t(p, j, k, core=1 - c).wait_recv()

    def consume(j, k):
        sib_wait(j, k)

        def one_core(core, _):
            products(j, k, core)
            return 0

        lax.fori_loop(0, 2, one_core, 0)

    def rowsum(value):
        return jnp.sum(value, axis=1, keepdims=True)

    def to_tp(d):
        return (ph, (tp + d) % 16)

    def to_ph(d):
        return ((ph + d) % 8, tp)

    def exchange(buf, slot, count, number, to):
        def copy(d):
            return remote(buf.at[slot], buf.at[slot], ex_s.at[number, d], ex_r.at[number, d], to(d))

        def start():
            for d in range(1, count):
                copy(d).start()

        def wait():
            for d in range(1, count):
                copy(d).wait_recv()

        def sent():
            for d in range(1, count):
                copy(d).wait_send()

        return start, wait, sent

    early_tp = exchange(ex_tp0, tp, 16, 0, to_tp)
    early_ph = exchange(ex_ph0, ph, 8, 1, to_ph)
    late_tp = exchange(ex_tp1, tp, 16, 2, to_tp)
    late_ph = exchange(ex_ph1, ph, 8, 3, to_ph)
    gain_ph = exchange(ex_gain, ph, 8, 4, to_ph)

    def to_columns(rows):
        filled = jnp.concatenate(rows + [jnp.zeros((128 - len(rows), TOKENS), F32)], axis=0)
        return jnp.transpose(filled)

    for i in range(3):
        for p in PARTS:
            p1(p, i).start()
    for p in PARTS:
        p2(p, 0, 0).start()
        p2(p, 0, 1).start()
    st[...] = jnp.broadcast_to(rowsum(wide * wide), st.shape)
    squares = jnp.transpose(st[...])[0:1]
    ex_tp0[tp] = jnp.concatenate(
        [squares[:, 128 * i : 128 * i + 128] for i in range(4)]
        + [s_gain[...].astype(F32), jnp.zeros((2, 128), F32)],
        axis=0,
    )
    lab[...] = to_columns([labels[...].astype(F32)])
    acc_t[...] = jnp.zeros_like(acc_t)
    for n in (1, 2, 3):
        for p in PARTS:
            a, b, d = ORDER[p]
            ref = block(p, rel(a, STEP[n]), me[b], me[d], PART[p])
            remote(ref, ref, s1.at[p, (1, 0, 2)[n - 1]], r1.at[p, (1, 0, 2)[n - 1]], sib).wait_recv()
            p2(p, n, 0).start()
            p2(p, n, 1).start()
    p3t_send(0)
    for p in PARTS:
        sib_t(p, 0, 0).start()
    for i in (0, 1):
        for p in PARTS:
            for n in range(4):
                p2_wait(p, n, i)
            p2f(p, i).start()
            sib_t(p, i + 1, 0).start()
    for p in PARTS:
        p2f_wait(p, 0)
        p2f_wait(p, 1)
        p3s(p, 0).start()
        p3s(p, 1).start()
        sib_t(p, 3, 0).start()
    p3t_send(1)
    early_tp[0]()
    ws_load.wait()
    ws_push = remote(ws, ws_sib, misc_s.at[0], misc_r.at[0], sib)
    ws_push.start()
    for load in wt_loads:
        load.wait()
    consume(0, 0)

    def forward(j):
        for i in (0, 1):
            for p in PARTS:
                p3t_wait(p, j, i)
                p3t(p, j, i + 2).start()
                sib_t(p, j, i + 1).start()

    def opposite(j):
        for p in PARTS:
            p3t_wait(p, j, 2)
            p3t_wait(p, j, 3)
            sib_t(p, j, 3).start()

    forward(0)
    p3t_send(2)
    consume(1, 0)
    consume(2, 0)
    early_tp[1]()
    early = ex_tp0[0]
    for i in range(1, 16):
        early = early + ex_tp0[i]
    ex_ph0[ph] = early
    early_ph[0]()
    for i in (0, 1):
        for p in PARTS:
            p3s_wait(p, i)
            p3s(p, i + 2).start()
    consume(3, 0)
    consume(0, 1)
    consume(0, 2)
    forward(1)
    p3t_send(3)
    consume(1, 1)
    for p in PARTS:
        p3s_wait(p, 2)
        p3s_wait(p, 3)
        sib_s(p, c).start()
    opposite(0)
    consume(1, 2)
    early_ph[1]()
    early = ex_ph0[0]
    for i in range(1, 8):
        early = early + ex_ph0[i]
    teacher_scale = lax.rsqrt(jnp.concatenate([early[i : i + 1] for i in range(4)], axis=1) / DT + NORM_EPSILON)
    col[...] = to_columns([teacher_scale])
    for p in PARTS:
        sib_s(p, 1 - c).wait_recv()

    def slab(q):
        return pl.ds(pl.multiple_of(q * SLAB, SLAB), SLAB)

    def halves(q, z, y):
        ref = G.at[q % 2, q // 2, z, y]
        first = jnp.concatenate([ref[0:48, :], ref[208:224, :]], axis=0)
        second = jnp.concatenate([ref[224:256, :], ref[416:448, :]], axis=0)
        return first.astype(F32), second.astype(F32)

    def norm_slab(q, _):
        def squares(z, total):
            for y in range(4):
                first, second = halves(q, z, y)
                total = total + (first * first + second * second)
            return total

        total = lax.fori_loop(0, 4, squares, jnp.zeros((SLAB, 128), F32))
        scale = lax.rsqrt(rowsum(total) / DS + NORM_EPSILON)
        rows = slab(q)
        scale_s[rows, :] = scale
        wide_scale = jnp.broadcast_to(scale, (SLAB, 128))

        def normed(z, _):
            for y in range(4):
                t = 4 * z + y
                first, second = halves(q, z, y)
                xs[t, rows, 0:128] = (first * wide_scale * ex_tp0[t, 4:5, :]).astype(BF16)
                xs[t, rows, 128:256] = (second * wide_scale * ex_tp0[t, 5:6, :]).astype(BF16)
            return 0

        lax.fori_loop(0, 4, normed, 0)
        return 0

    lax.fori_loop(0, 4, norm_slab, 0)
    forward(2)
    lax.fori_loop(4, 8, norm_slab, 0)

    def student_dot(t):
        lhs = jnp.concatenate([xs[2 * t], xs[2 * t + 1]], axis=1)
        rhs = jnp.concatenate([ws[2 * t], ws[2 * t + 1]], axis=0)
        return jnp.dot(lhs, rhs, preferred_element_type=F32)

    def student_dots(t, _):
        sl[...] += student_dot(t)
        return 0

    def nt_dot(lhs, rhs):
        return lax.dot_general(lhs, rhs, (((1,), (1,)), ((), ())), preferred_element_type=F32)

    eye = (
        lax.broadcasted_iota(jnp.int32, (256, 256), 0) == lax.broadcasted_iota(jnp.int32, (256, 256), 1)
    ).astype(F32).astype(BF16)

    def xst_copy(t):
        return pltpu.make_async_copy(xst.at[t % 2], xst_out.at[t], out_sem.at[t % 2])

    def turn(t, _):
        @pl.when(t >= 2)
        def _():
            xst_copy(t - 2).wait()

        xst[t % 2] = nt_dot(eye, xs[t]).astype(BF16)
        xst_copy(t).start()
        return 0

    sl[...] = student_dot(0)
    lax.fori_loop(1, 8, student_dots, 0)
    opposite(1)
    consume(0, 3)
    lane = lax.broadcasted_iota(jnp.int32, (SLAB, 128), 1)
    vocab_first = ((ph * 16 + tp) * LOCAL_V).astype(F32)

    def label_hit(rows):
        ids = lax.broadcasted_iota(jnp.int32, (SLAB, LOCAL_V), 1).astype(F32) + vocab_first
        return lab[rows, 0:1] == ids

    def pack(columns, first, out):
        for i, column in enumerate(columns):
            out = jnp.where(lane == first + i, column, out)
        return out

    def student_stats(q, _):
        rows = slab(q)
        logits = sl[rows, :]
        top = jnp.max(logits, axis=1, keepdims=True)
        e = jnp.exp(logits - top)
        es[rows, :] = e
        picked = jnp.where(label_hit(rows), logits, 0.0)
        st[rows, :] = pack(
            [top, rowsum(e), rowsum(e * logits), rowsum(picked)], 4, jnp.zeros((SLAB, 128), F32)
        )
        return 0

    lax.fori_loop(0, 8, student_stats, 0)
    consume(2, 1)
    consume(2, 2)
    forward(3)
    lax.fori_loop(0, 16, turn, 0)
    consume(1, 3)
    opposite(2)
    consume(3, 1)
    consume(3, 2)
    consume(2, 3)
    opposite(3)
    products(3, 3, c)
    sib_wait(3, 3)
    products(3, 3, 1 - c)

    def teacher_stats(q, _):
        rows = slab(q)
        logits = acc_t[rows, :] * col[rows, 0:1]
        student = sl[rows, :]
        top = jnp.max(logits, axis=1, keepdims=True)
        e = jnp.exp(logits - top)
        acc_t[rows, :] = e
        st[rows, :] = pack([top, rowsum(e), rowsum(e * (logits - student)), rowsum(e * student)], 0, st[rows, :])
        return 0

    lax.fori_loop(0, 8, teacher_stats, 0)
    stats = jnp.transpose(st[...])[0:8, :]
    sub = lax.broadcasted_iota(jnp.int32, (8, TOKENS), 0)

    def merge(buf, count):
        t_top, s_top = buf[0, 0:1, :], buf[0, 4:5, :]
        for i in range(1, count):
            t_top = jnp.maximum(t_top, buf[i, 0:1, :])
            s_top = jnp.maximum(s_top, buf[i, 4:5, :])
        total = jnp.zeros((8, TOKENS), F32)
        for i in range(count):
            weight = jnp.where(sub < 4, jnp.exp(buf[i, 0:1, :] - t_top), jnp.exp(buf[i, 4:5, :] - s_top))
            total = total + buf[i] * jnp.where(sub == 7, 1.0, weight)
        return jnp.where(sub == 0, t_top, jnp.where(sub == 4, s_top, total))

    ex_tp1[tp] = stats
    late_tp[0]()
    late_tp[1]()
    ex_ph1[ph] = merge(ex_tp1, 16)
    late_ph[0]()
    late_ph[1]()
    late = merge(ex_ph1, 8)
    teacher_top, teacher_total, student_top, student_total = late[0:1], late[1:2], late[4:5], late[5:6]
    picked_all = late[7:8]
    teacher_lse = teacher_top + jnp.log(teacher_total)
    student_lse = student_top + jnp.log(student_total)
    loss = (
        late[2:3] / teacher_total - teacher_lse + student_lse + LABEL_WEIGHT * (student_lse - picked_all)
    )
    inner = (
        (1.0 + LABEL_WEIGHT) * late[6:7] / student_total - late[3:4] / teacher_total - LABEL_WEIGHT * picked_all
    )
    t_factor = jnp.exp(stats[0:1] - teacher_top) / teacher_total
    s_factor = (1.0 + LABEL_WEIGHT) * jnp.exp(stats[4:5] - student_top) / student_total
    col[...] = to_columns([t_factor, s_factor, inner])

    def logit_grad(n, which):
        q = 2 * n + (c if which == 0 else 1 - c)
        rows = slab(q)
        g = (
            es[rows, :] * col[rows, 1:2]
            - acc_t[rows, :] * col[rows, 0:1]
            - LABEL_WEIGHT * label_hit(rows).astype(F32)
        ).astype(BF16)
        g_ref[rows, :] = g
        gp[which, slab(n), :] = g

    for which in (1, 0):

        def grad_step(n, _, which=which):
            logit_grad(n, which)
            return 0

        lax.fori_loop(0, 4, grad_step, 0)
        if which == 1:
            gp_push = remote(gp.at[1], gp_in, misc_s.at[1], misc_r.at[1], sib)
            gp_push.start()
    g_copy = pltpu.make_async_copy(g_ref, g_out, out_sem.at[2])
    g_copy.start()

    def own_first(t, _):
        r = nt_dot(gp[0], ws[t])
        for xt in range(4):
            own[xt, t // 4, t % 4, 0:64] = r[xt * 64 : xt * 64 + 64, 0:128]
            own[xt, t // 4, t % 4, 64:128] = r[xt * 64 : xt * 64 + 64, 128:256]
        return 0

    def own_second(t, _):
        r = nt_dot(gp_in[...], ws_sib[t])
        for xt in range(4):
            for h in range(2):
                at = pl.ds(64 * h, 64)
                total = own[xt, t // 4, t % 4, at, :] + r[xt * 64 : xt * 64 + 64, 128 * h : 128 * h + 128]
                own[xt, t // 4, t % 4, at, :] = total
                wt[xt, 0, t // 4, t % 4, at, 0:128] = total.astype(BF16)
        return 0

    lax.fori_loop(0, 16, own_first, 0)
    ws_push.wait_recv()
    gp_push.wait_recv()
    lax.fori_loop(0, 16, own_second, 0)

    def at3(p, one, two, three):
        a, b, d = ORDER[p]
        at = {a: one, b: two, d: three}
        return at["x"], at["z"], at["y"]

    def rest(p, two, three):
        at = {ORDER[p][1]: two, ORDER[p][2]: three}
        return tuple(at[axis] for axis in ("x", "z", "y") if axis in at)

    def stage_ref(p, one, two, three):
        ix, iz, iy = at3(p, one, two, three)
        return wt.at[ix, 0, iz, iy, pl.ds(*RS_PART[p]), pl.ds(0, 128)]

    def own_ref(p, one, two, three):
        ix, iz, iy = at3(p, one, two, three)
        return own.at[ix, iz, iy, pl.ds(*RS_PART[p]), :]

    HOP = (2, 1, -1)
    SUBSET = (2, 1, -1, 0)

    def rs1(p, k, i):
        a, b, d = ORDER[p]
        two = rel(b, SUBSET[k])
        src = stage_ref(p, rel(a, HOP[i]), two, ALL)
        dst = rs_b.at[(i, *rest(p, two, ALL), pl.ds(*RS_PART[p]), ALL)]
        return remote(src, dst, rs_s.at[p, 3 * k + i], rs_r.at[p, 3 * k + i], near(a, HOP[i]))

    def rs1_wait(p, k, i):
        dst = rs_b.at[(i, *rest(p, rel(ORDER[p][1], SUBSET[k]), ALL), pl.ds(*RS_PART[p]), ALL)]
        remote(dst, dst, rs_s.at[p, 3 * k + i], rs_r.at[p, 3 * k + i], sib).wait_recv()

    def rs2(p, i):
        a, b, d = ORDER[p]
        src = stage_ref(p, me[a], rel(b, HOP[i]), ALL)
        dst = rs_c.at[i, :, pl.ds(*RS_PART[p]), :]
        return remote(src, dst, rs_s.at[p, 12 + i], rs_r.at[p, 12 + i], near(b, HOP[i]))

    def rs3(p, i):
        a, b, d = ORDER[p]
        src = stage_ref(p, me[a], me[b], rel(d, HOP[i]))
        dst = rs_d.at[i, pl.ds(*RS_PART[p]), :]
        return remote(src, dst, rs_s.at[p, 15 + i], rs_r.at[p, 15 + i], near(d, HOP[i]))

    for k in range(4):
        for p in PARTS:
            for i in range(3):
                rs1(p, k, i).start()
    for k in range(4):
        for p in PARTS:
            rows = pl.ds(*RS_PART[p])
            for i in range(3):
                rs1_wait(p, k, i)

            def add_first(n, _, p=p, k=k, rows=rows):
                two = rel(ORDER[p][1], SUBSET[k])
                ref = own_ref(p, me[ORDER[p][0]], two, n)
                total = ref[...]
                for i in range(3):
                    total = total + rs_b[(i, *rest(p, two, n), rows, ALL)].astype(F32)
                if k == 3:
                    ref[...] = total
                else:
                    stage_ref(p, me[ORDER[p][0]], two, n)[...] = total.astype(BF16)
                return 0

            lax.fori_loop(0, 4, add_first, 0)
            if k < 3:
                rs2(p, k).start()
    for p in PARTS:
        rows = pl.ds(*RS_PART[p])
        for i in range(3):
            rs2(p, i).wait_recv()

        def add_second(n, _, p=p, rows=rows):
            ref = own_ref(p, me[ORDER[p][0]], me[ORDER[p][1]], n)
            total = ref[...]
            for i in range(3):
                total = total + rs_c[i, n, rows, :].astype(F32)
            ref[...] = total
            stage_ref(p, me[ORDER[p][0]], me[ORDER[p][1]], n)[...] = total.astype(BF16)
            return 0

        lax.fori_loop(0, 4, add_second, 0)
        for i in range(3):
            rs3(p, i).start()
    for p in PARTS:
        rows = pl.ds(*RS_PART[p])
        for i in range(3):
            rs3(p, i).wait_recv()
        total = own_ref(p, *own_at(p))[...]
        for i in range(3):
            total = total + rs_d[i, rows, :].astype(F32)
        fin[rows, :] = total

    rows = slab(ph)
    scale = scale_s[rows, :]
    raw = s_rows[...].astype(F32)
    gain = s_gain[...].astype(F32)
    sums = []
    for h in range(2):
        sums.append(rowsum_tokens(fin[h * 64 : h * 64 + 64, :] * raw[:, h * 128 : h * 128 + 128] * scale))
    ex_gain[ph] = jnp.broadcast_to(jnp.concatenate(sums, axis=1), (8, 256))
    gain_ph[0]()
    coefficient = scale * scale * col[rows, 2:3] / DS
    for h in range(2):
        cols = pl.ds(h * 128, 128)
        grad = fin[h * 64 : h * 64 + 64, :]
        rows_out[:, cols] = (scale * gain[h : h + 1] * grad - raw[:, h * 128 : h * 128 + 128] * coefficient).astype(BF16)
    sl[0:8, :] = jnp.broadcast_to(loss, (8, TOKENS))
    window = sl[0:1, pl.ds(pl.multiple_of(me["x"] * 128, 128), 128)]
    loss_out[...] = jnp.where(c == 1, window[:, 64:128], window[:, 0:64])

    for p in PARTS:
        for i in range(3):
            p1(p, i).wait_send()
        for i in range(8):
            p2(p, i // 2, i % 2).wait_send()
        for i in range(2):
            p2f(p, i).wait_send()
        for i in range(4):
            p3s(p, i).wait_send()
        sib_s(p, c).wait_send()
        for j in range(4):
            for i in range(4):
                p3t(p, j, i).wait_send()
                sib_t(p, j, i).wait_send()
        for i in range(3):
            for k in range(4):
                rs1(p, k, i).wait_send()
            rs2(p, i).wait_send()
            rs3(p, i).wait_send()
    for ex in (early_tp, early_ph, late_tp, late_ph):
        ex[2]()
    ws_push.wait_send()
    gp_push.wait_send()
    xst_copy(14).wait()
    xst_copy(15).wait()
    g_copy.wait()
    gain_ph[1]()
    total = ex_gain[0]
    for i in range(1, 8):
        total = total + ex_gain[i]
    gain_out[...] = total[0:1]
    gain_ph[2]()


def rowsum_tokens(value):
    return jnp.sum(value, axis=0, keepdims=True)


def head_kernel(xst_ref, g_ref, out_ref):
    out_ref[...] = jnp.dot(
        xst_ref[...].reshape(512, TOKENS), g_ref[...], preferred_element_type=F32
    ).astype(BF16)


def local(teacher_rows, teacher_gain, teacher_head, student_rows, student_gain, student_head, labels):
    vmem = pl.BlockSpec(memory_space=pltpu.VMEM)
    hbm = pl.BlockSpec(memory_space=pl.ANY)
    dma = pltpu.SemaphoreType.DMA
    loss, rows_grad, gain_grad, xst, g = pl.pallas_call(
        comm_kernel,
        out_shape=(
            jax.ShapeDtypeStruct((1, SLAB), F32),
            jax.ShapeDtypeStruct((SLAB, 256), BF16),
            jax.ShapeDtypeStruct((1, 256), F32),
            jax.ShapeDtypeStruct((16, 256, TOKENS), BF16),
            jax.ShapeDtypeStruct((TOKENS, LOCAL_V), BF16),
        ),
        in_specs=[vmem, vmem, hbm, vmem, vmem, hbm, vmem],
        out_specs=(vmem, vmem, vmem, hbm, hbm),
        scratch_shapes=[
            pltpu.VMEM((2, 4, 4, 4, 640, 128), BF16),
            pltpu.VMEM((4, 2, 4, 4, 128, LOCAL_V), BF16),
            pltpu.VMEM((16, 256, LOCAL_V), BF16),
            pltpu.VMEM((16, 256, LOCAL_V), BF16),
            pltpu.VMEM((16, TOKENS, 256), BF16),
            pltpu.VMEM((2, 256, TOKENS), BF16),
            pltpu.VMEM((TOKENS, LOCAL_V), F32),
            pltpu.VMEM((TOKENS, LOCAL_V), F32),
            pltpu.VMEM((TOKENS, LOCAL_V), F32),
            pltpu.VMEM((TOKENS, 128), F32),
            pltpu.VMEM((TOKENS, 128), F32),
            pltpu.VMEM((TOKENS, 128), F32),
            pltpu.VMEM((TOKENS, 1), F32),
            pltpu.VMEM((TOKENS, LOCAL_V), BF16),
            pltpu.VMEM((2, 256, LOCAL_V), BF16),
            pltpu.VMEM((256, LOCAL_V), BF16),
            pltpu.VMEM((4, 4, 4, 128, 128), F32),
            pltpu.VMEM((3, 4, 4, 128, 128), BF16),
            pltpu.VMEM((3, 4, 128, 128), BF16),
            pltpu.VMEM((3, 128, 128), BF16),
            pltpu.VMEM((128, 128), F32),
            pltpu.VMEM((16, 8, 128), F32),
            pltpu.VMEM((8, 8, 128), F32),
            pltpu.VMEM((16, 8, TOKENS), F32),
            pltpu.VMEM((8, 8, TOKENS), F32),
            pltpu.VMEM((8, 8, 256), F32),
            dma((5,)), dma((3,)),
            dma((3, 3)), dma((3, 3)), dma((3, 8)), dma((3, 8)), dma((3, 2)), dma((3, 2)),
            dma((3, 4)), dma((3, 4)), dma((3, 16)), dma((3, 16)), dma((3,)), dma((3,)), dma((3, 16)), dma((3, 16)),
            dma((5, 16)), dma((5, 16)), dma((2,)), dma((2,)), dma((3, 18)), dma((3, 18)),
        ],
        compiler_params=pltpu.CompilerParams(
            collective_id=0, has_side_effects=True, vmem_limit_bytes=63 << 20
        ),
        name="distill",
    )(
        teacher_rows,
        teacher_gain.reshape(1, 128),
        teacher_head.reshape(4, 2, 4, 4, 128, LOCAL_V),
        student_rows,
        student_gain.reshape(2, 128),
        student_head.reshape(16, 256, LOCAL_V),
        labels.reshape(1, TOKENS),
    )
    head_grad = pl.pallas_call(
        head_kernel,
        grid=(8,),
        out_shape=jax.ShapeDtypeStruct((DS, LOCAL_V), BF16),
        in_specs=[
            pl.BlockSpec((2, 256, TOKENS), lambda t: (t, 0, 0)),
            pl.BlockSpec((TOKENS, LOCAL_V), lambda t: (0, 0)),
        ],
        out_specs=pl.BlockSpec((512, LOCAL_V), lambda t: (t, 0)),
        name="head_grad",
    )(xst, g)
    return loss.reshape(SLAB), head_grad, rows_grad, gain_grad.reshape(256)


def solution(mesh):
    placed = (
        P(None, ("phase", "tp")),
        P(("phase", "tp")),
        P(None, ("phase", "tp")),
        P("phase", "tp"),
        P("tp"),
        P(None, ("phase", "tp")),
        P(),
    )
    return jax.shard_map(
        local,
        mesh=mesh,
        in_specs=placed,
        out_specs=(P("phase"), P(None, ("phase", "tp")), P("phase", "tp"), P("tp")),
        check_vma=False,
    )
```

time: 516 us -> 130 us (0.25)
  blocking collectives: 289 us -> 0 us
  waiting for transfers between devices: 166 us -> 0 us
  Pallas kernels: 0 us -> 128 us
  matrix products: 36.1 us -> 0 us
  between operations: 13.8 us -> 0.67 us
  other arithmetic: 8.61 us -> 0 us
    psum x4 -> x0, blocking collectives: 189 us -> none  [the longest x1 68.6 us: local(): lax.psum(jnp.sum(teacher_wide * teacher_wide, axis=1), ('phase', 'tp'))]
    pallas_call x0 -> x2, Pallas kernels: none -> 128 us  [the longest x1 119 us: local(): pl.pallas_call(comm_kernel, out_shape=(jax.ShapeDtypeStruct((1, SLAB), F3...]
    reduce_scatter x2 -> x0, waiting for transfers between devices: 103 us -> none  [the longest x1 80.2 us: local(): lax.psum_scatter(lax.dot_general(head_rows, logit_grad, (((1,), (1,)), ((...]
    pmax x1 -> x0, blocking collectives: 64.6 us -> none  [local(): lax.pmax((jnp.max(teacher_logits, axis=1), jnp.max(student_logits, axis=1...]
    all_gather x2 -> x0, waiting for transfers between devices: 63 us -> none  [the longest x1 63 us: local(): lax.all_gather(teacher_scaled, ('phase', 'tp'), axis=1, tiled=True)]
    dot_general x4 -> x0, matrix products: 36.1 us -> none  [the longest x1 14.9 us: local(): jnp.dot(lax.all_gather(teacher_scaled, ('phase', 'tp'), axis=1, tiled=Tru...]
    all_gather x2 -> x0, blocking collectives: 35.9 us -> none  [the longest x1 20.1 us: local(): lax.all_gather(student_gain, 'tp', axis=0, tiled=True)]
    reduce_sum x4 -> x0, other arithmetic: 6.27 us -> none  [the longest x1 3.13 us: local(): jnp.mean(full_wide * full_wide, axis=1) + NORM_EPSILON]
  transfers between devices with their start and end apart: 4 -> 0, of which waited for: 3 -> 0; matrix products, arithmetic and copies ran while one was open for 4% -> 0% of each run, Pallas kernels for 0% -> 0%
where the time goes in v2:
time: 130 us
  Pallas kernels  128 us (98%)
  local copies, waits for them, and re-layouts  1.7 us (1%)
    pallas_call x1, Pallas kernels, local(): pl.pallas_call(comm_kernel, out_shape=(jax.ShapeDtypeStruct((1, SLAB), F3...  119 us
    pallas_call x1, Pallas kernels, local(): pl.pallas_call(head_kernel, grid=(8,), out_shape=jax.ShapeDtypeStruct((DS...  8.19 us

profile of v2, /device:TPU:1, one launch (start us, length us, event | category | flops | bytes accessed | tf_op | source)
XLA Modules:
  0.0 129.9 jit_solution(8226538002666562189)
XLA Ops:
  0.6 119.4 %distill.1 = (f32[1,64]{1,0:T(1,128)}, bf16[64,256]{1,0:T(8,128)(2,1)}, f32[1,256]{1,0:T(1,128)}, bf16[16,256,512]{2,1,0:T(8,128)(2,1)}, bf16[512,512]{1,0:T(8,128)(2,1)}) custom-call(bf16[512,128]{1,0:T(8,128)(2,1)} %t_rows.1, bf16[1,128]{1,0:T(2,128)(2,1)} %bitcast.11, bf16[4,2,4,4,128,512]{5,4,3,2,1,0:T(8,128)(2,1)} %bitcast.7, bf16[64,256]{1,0:T(8,128)(2,1)} %s_rows.1, ...), custom_call_target="tpu_custom_call" | custom-call | tf_op jit(solution)/shard_map/distill/pallas_call | solution.py:658
  120.0 0.0 copy-start.2
  120.0 0.0 copy-start
  120.0 0.0 copy-start.1
  120.0 8.2 %head_grad.1 = bf16[4096,512]{1,0:T(8,128)(2,1)} custom-call(bf16[16,256,512]{2,1,0:T(8,128)(2,1)} %get-tuple-element.10.xst_ref, bf16[512,512]{1,0:T(8,128)(2,1)} %get-tuple-element.11.g_ref), custom_call_target="tpu_custom_call" | custom-call | tf_op jit(solution)/shard_map/head_grad/pallas_call | solution.py:714
  128.2 0.0 copy-done.2
  128.2 0.5 copy.14
  128.7 0.0 copy-done
  128.8 0.6 copy.15
  129.4 0.0 copy-done.1
  129.4 0.6 copy.16
Async XLA Ops:
  120.0 8.2 %copy-start.2 = (f32[1,64]{1,0:T(1,128)S(1)}, f32[1,64]{1,0:T(1,128)}, u32[]{:S(2)}) copy-start(f32[1,64]{1,0:T(1,128)} %get-tuple-element.9) | copy-start | bytes 772
  120.0 8.7 %copy-start = (bf16[64,256]{1,0:T(8,128)(2,1)S(1)}, bf16[64,256]{1,0:T(8,128)(2,1)}, u32[]{:S(2)}) copy-start(bf16[64,256]{1,0:T(8,128)(2,1)} %get-tuple-element.20) | copy-start | bytes 98308
  120.0 9.3 %copy-start.1 = (f32[1,256]{1,0:T(1,128)S(1)}, f32[1,256]{1,0:T(1,128)}, u32[]{:S(2)}) copy-start(f32[1,256]{1,0:T(1,128)} %get-tuple-element.13) | copy-start | bytes 3076

commit v3 on v2

--- a/solution.py
+++ b/solution.py
@@ -26,10 +26,9 @@
 def comm_kernel(
     t_rows, t_gain, wt_hbm, s_rows, s_gain, ws_hbm, labels,
     loss_out, rows_out, gain_out, xst_out, g_out,
-    G, wt, ws, ws_sib, xs, xst, acc_t, sl, es, st, col, lab, scale_s, g_ref, gp, gp_in, own,
-    rs_b, rs_c, rs_d, fin, ex_tp0, ex_ph0, ex_tp1, ex_ph1, ex_gain,
-    w_sem, out_sem, s1, r1, s2, r2, s2f, r2f, s3s, r3s, s3t, r3t, sibs_s, sibs_r, sibt_s, sibt_r,
-    ex_s, ex_r, misc_s, misc_r, rs_s, rs_r,
+    G, wt, ws, ws_sib, xst, acc_t, sl, es, st, col, lab, scale_s, g_ref, gp, gp_in, own,
+    rs_b, rs_c, rs_d, fin, ex_y0, ex_z0, ex_ph0, ex_tp1, ex_ph1, ex_gain,
+    w_sem, out_sem, send, r1, r2, r2f, r1s, r2s, r3s, r3t, sibs_r, sibt_r, ex_s, ex_r, misc_s, misc_r, rs_r,
 ):
     ph = lax.axis_index("phase")
     tp = lax.axis_index("tp")
@@ -68,12 +67,6 @@
     scaled = (wide * t_gain[...].astype(F32)).astype(BF16)
     for (row, size), token in zip(PART_T, TOKEN_T):
         mine[pl.ds(row, size), :] = scaled[token : token + size]
-    srow = s_rows[...]
-    mine[0:48, :] = srow[0:48, 0:128]
-    mine[208:224, :] = srow[48:64, 0:128]
-    mine[224:256, :] = srow[0:32, 128:256]
-    mine[416:448, :] = srow[32:64, 128:256]
-
     pl.semaphore_wait(barrier, len(partners))
 
     def block(p, one, two, three, rows, core=None):
@@ -85,57 +78,74 @@
         return tuple(me[axis] for axis in ORDER[p])
 
     def p1(p, i):
-        ref = block(p, *own_at(p), PART[p])
-        return remote(ref, ref, s1.at[p, i], r1.at[p, i], near(ORDER[p][0], (-1, 1, 2)[i]))
+        ref = block(p, *own_at(p), PART_T[p])
+        return remote(ref, ref, send.at[p, 0], r1.at[p, i], near(ORDER[p][0], (-1, 1, 2)[i]))
 
     def p2(p, n, i):
         a, b, d = ORDER[p]
-        ref = block(p, rel(a, STEP[n]), me[b], me[d], PART[p])
-        return remote(ref, ref, s2.at[p, 2 * n + i], r2.at[p, 2 * n + i], near(b, (1, -1)[i]))
+        ref = block(p, rel(a, STEP[n]), me[b], me[d], PART_T[p])
+        return remote(ref, ref, send.at[p, 1], r2.at[p, i], near(b, (1, -1)[i]))
 
     def p2f(p, i):
         a, b, d = ORDER[p]
-        ref = block(p, (LOW, HIGH)[i], rel(b, (-1, 1)[i]), me[d], PART[p])
-        return remote(ref, ref, s2f.at[p, i], r2f.at[p, i], near(b, (1, -1)[i]))
+        ref = block(p, (LOW, HIGH)[i], rel(b, (-1, 1)[i]), me[d], PART_T[p])
+        return remote(ref, ref, send.at[p, 1], r2f.at[p, i], near(b, (1, -1)[i]))
+
+    def p1s(p, i):
+        ref = block(p, *own_at(p), PART_S[p])
+        return remote(ref, ref, send.at[p, 2], r1s.at[p, i], near(ORDER[p][0], (-1, 1, 2)[i]))
+
+    def p2s(p, i):
+        a, b, d = ORDER[p]
+        ref = block(p, ALL, me[b], me[d], PART_S[p])
+        return remote(ref, ref, send.at[p, 2], r2s.at[p, i], near(b, (-1, 1, 2)[i]))
 
     def p3s(p, i):
         d = ORDER[p][2]
         ref = block(p, (ALL, ALL, LOW, HIGH)[i], ALL, rel(d, (0, 0, -1, 1)[i]), PART_S[p])
-        return remote(ref, ref, s3s.at[p, i], r3s.at[p, i], near(d, (1, -1, 1, -1)[i]))
+        return remote(ref, ref, send.at[p, 2], r3s.at[p, i], near(d, (1, -1, 1, -1)[i]))
 
     def p3t(p, j, i):
         a, b, d = ORDER[p]
         ref = block(p, (ALL, ALL, LOW, HIGH)[i], rel(b, STEP[j]), rel(d, (0, 0, -1, 1)[i]), PART_T[p])
-        return remote(ref, ref, s3t.at[p, 4 * j + i], r3t.at[p, 4 * j + i], near(d, (1, -1, 1, -1)[i]))
-
-    def p2_wait(p, n, i):
-        a, b, d = ORDER[p]
-        ref = block(p, rel(a, STEP[n]), rel(b, (-1, 1)[i]), me[d], PART[p])
-        remote(ref, ref, s2.at[p, 2 * n + i], r2.at[p, 2 * n + i], sib).wait_recv()
+        return remote(ref, ref, send.at[p, 3], r3t.at[p, 4 * j + i], near(d, (1, -1, 1, -1)[i]))
+
+    def arrive(ref, sem):
+        pltpu.make_async_copy(ref, ref, sem).wait()
+
+    def p2_wait(p, i):
+        a, b, d = ORDER[p]
+        arrive(block(p, ALL, rel(b, (-1, 1)[i]), me[d], PART_T[p]), r2.at[p, i])
 
     def p2f_wait(p, i):
         a, b, d = ORDER[p]
-        ref = block(p, (LOW, HIGH)[i], rel(b, 2), me[d], PART[p])
-        remote(ref, ref, s2f.at[p, i], r2f.at[p, i], sib).wait_recv()
+        arrive(block(p, (LOW, HIGH)[i], rel(b, 2), me[d], PART_T[p]), r2f.at[p, i])
+
+    def p1s_wait(p, i):
+        a, b, d = ORDER[p]
+        arrive(block(p, rel(a, (1, -1, 2)[i]), me[b], me[d], PART_S[p]), r1s.at[p, i])
+
+    def p2s_wait(p, i):
+        a, b, d = ORDER[p]
+        arrive(block(p, ALL, rel(b, (1, -1, 2)[i]), me[d], PART_S[p]), r2s.at[p, i])
 
     def p3s_wait(p, i):
         d = ORDER[p][2]
-        ref = block(p, (ALL, ALL, LOW, HIGH)[i], ALL, rel(d, (-1, 1, 2, 2)[i]), PART_S[p])
-        remote(ref, ref, s3s.at[p, i], r3s.at[p, i], sib).wait_recv()
+        arrive(block(p, (ALL, ALL, LOW, HIGH)[i], ALL, rel(d, (-1, 1, 2, 2)[i]), PART_S[p]), r3s.at[p, i])
 
     def p3t_wait(p, j, i):
         a, b, d = ORDER[p]
         ref = block(p, (ALL, ALL, LOW, HIGH)[i], rel(b, STEP[j]), rel(d, (-1, 1, 2, 2)[i]), PART_T[p])
-        remote(ref, ref, s3t.at[p, 4 * j + i], r3t.at[p, 4 * j + i], sib).wait_recv()
+        arrive(ref, r3t.at[p, 4 * j + i])
 
     def sib_t(p, j, k, core=None):
         a, b, d = ORDER[p]
         ref = block(p, ALL, rel(b, STEP[j]), rel(d, STEP[k]), PART_T[p], core)
-        return remote(ref, ref, sibt_s.at[p, 4 * j + k], sibt_r.at[p, 4 * j + k], sib)
+        return remote(ref, ref, send.at[p, 4], sibt_r.at[p, 4 * j + k], sib)
 
     def sib_s(p, core):
         ref = G.at[core, :, :, :, pl.ds(*PART_S[p]), :]
-        return remote(ref, ref, sibs_s.at[p], sibs_r.at[p], sib)
+        return remote(ref, ref, send.at[p, 5], sibs_r.at[p], sib)
 
     def p3t_send(j):
         for p in PARTS:
@@ -153,7 +163,8 @@
 
     def sib_wait(j, k):
         for p in PARTS:
-            sib_t(p, j, k, core=1 - c).wait_recv()
+            a, b, d = ORDER[p]
+            arrive(block(p, ALL, rel(b, STEP[j]), rel(d, STEP[k]), PART_T[p], 1 - c), sibt_r.at[p, 4 * j + k])
 
     def consume(j, k):
         sib_wait(j, k)
@@ -175,7 +186,7 @@
 
     def exchange(buf, slot, count, number, to):
         def copy(d):
-            return remote(buf.at[slot], buf.at[slot], ex_s.at[number, d], ex_r.at[number, d], to(d))
+            return remote(buf.at[slot], buf.at[slot], ex_s.at[number], ex_r.at[number, d], to(d))
 
         def start():
             for d in range(1, count):
@@ -186,12 +197,12 @@
                 copy(d).wait_recv()
 
         def sent():
-            for d in range(1, count):
-                copy(d).wait_send()
+            arrive(buf.at[pl.ds(0, count - 1)], ex_s.at[number])
 
         return start, wait, sent
 
-    early_tp = exchange(ex_tp0, tp, 16, 0, to_tp)
+    early_y = exchange(ex_y0, me["y"], 4, 0, lambda d: near("y", d))
+    early_z = exchange(ex_z0, me["z"], 4, 5, lambda d: near("z", d))
     early_ph = exchange(ex_ph0, ph, 8, 1, to_ph)
     late_tp = exchange(ex_tp1, tp, 16, 2, to_tp)
     late_ph = exchange(ex_ph1, ph, 8, 3, to_ph)
@@ -207,44 +218,68 @@
     for p in PARTS:
         p2(p, 0, 0).start()
         p2(p, 0, 1).start()
-    st[...] = jnp.broadcast_to(rowsum(wide * wide), st.shape)
-    squares = jnp.transpose(st[...])[0:1]
-    ex_tp0[tp] = jnp.concatenate(
-        [squares[:, 128 * i : 128 * i + 128] for i in range(4)]
-        + [s_gain[...].astype(F32), jnp.zeros((2, 128), F32)],
+    raw = s_rows[...].astype(F32)
+    raw_squares = rowsum(raw * raw)
+    lane_t = lax.broadcasted_iota(jnp.int32, (TOKENS, 128), 1)
+    st[...] = jnp.where(lane_t == 0, rowsum(wide * wide), 0.0)
+    st[0:SLAB, :] = jnp.where(lane_t[0:SLAB] == 1, raw_squares, st[0:SLAB, :])
+    squares = jnp.transpose(st[...])
+    ex_y0[me["y"]] = jnp.concatenate(
+        [squares[0:1, 128 * i : 128 * i + 128] for i in range(4)]
+        + [squares[1:2, 0:128], jnp.zeros((3, 128), F32)],
         axis=0,
     )
+    early_y[0]()
     lab[...] = to_columns([labels[...].astype(F32)])
     acc_t[...] = jnp.zeros_like(acc_t)
     for n in (1, 2, 3):
         for p in PARTS:
             a, b, d = ORDER[p]
-            ref = block(p, rel(a, STEP[n]), me[b], me[d], PART[p])
-            remote(ref, ref, s1.at[p, (1, 0, 2)[n - 1]], r1.at[p, (1, 0, 2)[n - 1]], sib).wait_recv()
+            arrive(block(p, rel(a, STEP[n]), me[b], me[d], PART_T[p]), r1.at[p, (1, 0, 2)[n - 1]])
             p2(p, n, 0).start()
             p2(p, n, 1).start()
     p3t_send(0)
+    early_y[1]()
+    ex_z0[me["z"]] = ex_y0[0] + ex_y0[1] + ex_y0[2] + ex_y0[3]
+    early_z[0]()
     for p in PARTS:
         sib_t(p, 0, 0).start()
     for i in (0, 1):
         for p in PARTS:
-            for n in range(4):
-                p2_wait(p, n, i)
+            p2_wait(p, i)
             p2f(p, i).start()
             sib_t(p, i + 1, 0).start()
+    early_z[1]()
+    early = ex_z0[0] + ex_z0[1] + ex_z0[2] + ex_z0[3]
+    ex_ph0[ph] = early
+    turned = jnp.transpose(jnp.concatenate([early, jnp.zeros((120, 128), F32)], axis=0))
+    own_scale = lax.rsqrt(turned[0:SLAB, 4:5] / DS + NORM_EPSILON)
+    scale_s[...] = own_scale
+    gain = s_gain[...].astype(F32)
+    left = (raw[:, 0:128] * own_scale * gain[0:1]).astype(BF16)
+    right = (raw[:, 128:256] * own_scale * gain[1:2]).astype(BF16)
+    mine[0:48, :] = left[0:48]
+    mine[208:224, :] = left[48:64]
+    mine[224:256, :] = right[0:32]
+    mine[416:448, :] = right[32:64]
+    for i in range(3):
+        for p in PARTS:
+            p1s(p, i).start()
     for p in PARTS:
         p2f_wait(p, 0)
         p2f_wait(p, 1)
-        p3s(p, 0).start()
-        p3s(p, 1).start()
         sib_t(p, 3, 0).start()
     p3t_send(1)
-    early_tp[0]()
     ws_load.wait()
     ws_push = remote(ws, ws_sib, misc_s.at[0], misc_r.at[0], sib)
     ws_push.start()
     for load in wt_loads:
         load.wait()
+    for p in PARTS:
+        for i in range(3):
+            p1s_wait(p, i)
+        for i in range(3):
+            p2s(p, i).start()
     consume(0, 0)
 
     def forward(j):
@@ -261,31 +296,26 @@
             sib_t(p, j, 3).start()
 
     forward(0)
+    consume(1, 0)
+    for p in PARTS:
+        for i in range(3):
+            p2s_wait(p, i)
+        p3s(p, 0).start()
+        p3s(p, 1).start()
     p3t_send(2)
-    consume(1, 0)
+    early_ph[0]()
     consume(2, 0)
-    early_tp[1]()
-    early = ex_tp0[0]
-    for i in range(1, 16):
-        early = early + ex_tp0[i]
-    ex_ph0[ph] = early
-    early_ph[0]()
+    consume(3, 0)
+    forward(1)
     for i in (0, 1):
         for p in PARTS:
             p3s_wait(p, i)
             p3s(p, i + 2).start()
-    consume(3, 0)
+    p3t_send(3)
     consume(0, 1)
     consume(0, 2)
-    forward(1)
-    p3t_send(3)
+    opposite(0)
     consume(1, 1)
-    for p in PARTS:
-        p3s_wait(p, 2)
-        p3s_wait(p, 3)
-        sib_s(p, c).start()
-    opposite(0)
-    consume(1, 2)
     early_ph[1]()
     early = ex_ph0[0]
     for i in range(1, 8):
@@ -293,52 +323,35 @@
     teacher_scale = lax.rsqrt(jnp.concatenate([early[i : i + 1] for i in range(4)], axis=1) / DT + NORM_EPSILON)
     col[...] = to_columns([teacher_scale])
     for p in PARTS:
-        sib_s(p, 1 - c).wait_recv()
+        p3s_wait(p, 2)
+        p3s_wait(p, 3)
+        sib_s(p, c).start()
+    consume(1, 2)
+    consume(0, 3)
+    for p in PARTS:
+        arrive(G.at[1 - c, :, :, :, pl.ds(*PART_S[p]), :], sibs_r.at[p])
 
     def slab(q):
         return pl.ds(pl.multiple_of(q * SLAB, SLAB), SLAB)
 
-    def halves(q, z, y):
-        ref = G.at[q % 2, q // 2, z, y]
-        first = jnp.concatenate([ref[0:48, :], ref[208:224, :]], axis=0)
-        second = jnp.concatenate([ref[224:256, :], ref[416:448, :]], axis=0)
-        return first.astype(F32), second.astype(F32)
-
-    def norm_slab(q, _):
-        def squares(z, total):
-            for y in range(4):
-                first, second = halves(q, z, y)
-                total = total + (first * first + second * second)
-            return total
-
-        total = lax.fori_loop(0, 4, squares, jnp.zeros((SLAB, 128), F32))
-        scale = lax.rsqrt(rowsum(total) / DS + NORM_EPSILON)
-        rows = slab(q)
-        scale_s[rows, :] = scale
-        wide_scale = jnp.broadcast_to(scale, (SLAB, 128))
-
-        def normed(z, _):
-            for y in range(4):
-                t = 4 * z + y
-                first, second = halves(q, z, y)
-                xs[t, rows, 0:128] = (first * wide_scale * ex_tp0[t, 4:5, :]).astype(BF16)
-                xs[t, rows, 128:256] = (second * wide_scale * ex_tp0[t, 5:6, :]).astype(BF16)
-            return 0
-
-        lax.fori_loop(0, 4, normed, 0)
-        return 0
-
-    lax.fori_loop(0, 4, norm_slab, 0)
-    forward(2)
-    lax.fori_loop(4, 8, norm_slab, 0)
-
-    def student_dot(t):
-        lhs = jnp.concatenate([xs[2 * t], xs[2 * t + 1]], axis=1)
-        rhs = jnp.concatenate([ws[2 * t], ws[2 * t + 1]], axis=0)
+    def normed(z, y):
+        slabs = []
+        for q in range(8):
+            ref = G.at[q % 2, q // 2, z, y]
+            first = jnp.concatenate([ref[0:48, :], ref[208:224, :]], axis=0)
+            second = jnp.concatenate([ref[224:256, :], ref[416:448, :]], axis=0)
+            slabs.append(jnp.concatenate([first, second], axis=1))
+        return jnp.concatenate(slabs, axis=0)
+
+    def student_dot(z, half):
+        t = 4 * z + 2 * half
+        lhs = jnp.concatenate([normed(z, 2 * half), normed(z, 2 * half + 1)], axis=1)
+        rhs = jnp.concatenate([ws[t], ws[t + 1]], axis=0)
         return jnp.dot(lhs, rhs, preferred_element_type=F32)
 
-    def student_dots(t, _):
-        sl[...] += student_dot(t)
+    def student_dots(z, _):
+        sl[...] += student_dot(z, 0)
+        sl[...] += student_dot(z, 1)
         return 0
 
     def nt_dot(lhs, rhs):
@@ -351,19 +364,26 @@
     def xst_copy(t):
         return pltpu.make_async_copy(xst.at[t % 2], xst_out.at[t], out_sem.at[t % 2])
 
-    def turn(t, _):
-        @pl.when(t >= 2)
-        def _():
-            xst_copy(t - 2).wait()
-
-        xst[t % 2] = nt_dot(eye, xs[t]).astype(BF16)
-        xst_copy(t).start()
+    def turn(z, _):
+        for y in range(4):
+            t = 4 * z + y
+            if y >= 2:
+                xst_copy(t - 2).wait()
+            else:
+
+                @pl.when(z >= 1)
+                def _(t=t):
+                    xst_copy(t - 2).wait()
+
+            xst[t % 2] = nt_dot(eye, normed(z, y)).astype(BF16)
+            xst_copy(t).start()
         return 0
 
-    sl[...] = student_dot(0)
-    lax.fori_loop(1, 8, student_dots, 0)
+    sl[...] = student_dot(0, 0)
+    sl[...] += student_dot(0, 1)
+    forward(2)
+    lax.fori_loop(1, 4, student_dots, 0)
     opposite(1)
-    consume(0, 3)
     lane = lax.broadcasted_iota(jnp.int32, (SLAB, 128), 1)
     vocab_first = ((ph * 16 + tp) * LOCAL_V).astype(F32)
 
@@ -392,7 +412,6 @@
     consume(2, 1)
     consume(2, 2)
     forward(3)
-    lax.fori_loop(0, 16, turn, 0)
     consume(1, 3)
     opposite(2)
     consume(3, 1)
@@ -473,27 +492,27 @@
     g_copy = pltpu.make_async_copy(g_ref, g_out, out_sem.at[2])
     g_copy.start()
 
-    def own_first(t, _):
-        r = nt_dot(gp[0], ws[t])
-        for xt in range(4):
-            own[xt, t // 4, t % 4, 0:64] = r[xt * 64 : xt * 64 + 64, 0:128]
-            own[xt, t // 4, t % 4, 64:128] = r[xt * 64 : xt * 64 + 64, 128:256]
+    def own_first(z, _):
+        for y in range(4):
+            r = nt_dot(gp[0], ws[4 * z + y])
+            for xt in range(4):
+                own[xt, z, y, 0:64] = r[xt * 64 : xt * 64 + 64, 0:128]
+                own[xt, z, y, 64:128] = r[xt * 64 : xt * 64 + 64, 128:256]
         return 0
 
-    def own_second(t, _):
-        r = nt_dot(gp_in[...], ws_sib[t])
-        for xt in range(4):
-            for h in range(2):
-                at = pl.ds(64 * h, 64)
-                total = own[xt, t // 4, t % 4, at, :] + r[xt * 64 : xt * 64 + 64, 128 * h : 128 * h + 128]
-                own[xt, t // 4, t % 4, at, :] = total
-                wt[xt, 0, t // 4, t % 4, at, 0:128] = total.astype(BF16)
-        return 0
-
-    lax.fori_loop(0, 16, own_first, 0)
+    def own_second(z):
+        for y in range(4):
+            r = nt_dot(gp_in[...], ws_sib[4 * z + y])
+            for xt in range(4):
+                for h in range(2):
+                    at = pl.ds(64 * h, 64)
+                    total = own[xt, z, y, at, :] + r[xt * 64 : xt * 64 + 64, 128 * h : 128 * h + 128]
+                    own[xt, z, y, at, :] = total
+                    wt[xt, 0, z, y, at, 0:128] = total.astype(BF16)
+
+    lax.fori_loop(0, 4, own_first, 0)
     ws_push.wait_recv()
     gp_push.wait_recv()
-    lax.fori_loop(0, 16, own_second, 0)
 
     def at3(p, one, two, three):
         a, b, d = ORDER[p]
@@ -520,28 +539,35 @@
         two = rel(b, SUBSET[k])
         src = stage_ref(p, rel(a, HOP[i]), two, ALL)
         dst = rs_b.at[(i, *rest(p, two, ALL), pl.ds(*RS_PART[p]), ALL)]
-        return remote(src, dst, rs_s.at[p, 3 * k + i], rs_r.at[p, 3 * k + i], near(a, HOP[i]))
+        return remote(src, dst, send.at[p, 6], rs_r.at[p, 3 * k + i], near(a, HOP[i]))
 
     def rs1_wait(p, k, i):
         dst = rs_b.at[(i, *rest(p, rel(ORDER[p][1], SUBSET[k]), ALL), pl.ds(*RS_PART[p]), ALL)]
-        remote(dst, dst, rs_s.at[p, 3 * k + i], rs_r.at[p, 3 * k + i], sib).wait_recv()
+        arrive(dst, rs_r.at[p, 3 * k + i])
 
     def rs2(p, i):
         a, b, d = ORDER[p]
         src = stage_ref(p, me[a], rel(b, HOP[i]), ALL)
         dst = rs_c.at[i, :, pl.ds(*RS_PART[p]), :]
-        return remote(src, dst, rs_s.at[p, 12 + i], rs_r.at[p, 12 + i], near(b, HOP[i]))
+        return remote(src, dst, send.at[p, 7], rs_r.at[p, 12 + i], near(b, HOP[i]))
 
     def rs3(p, i):
         a, b, d = ORDER[p]
         src = stage_ref(p, me[a], me[b], rel(d, HOP[i]))
         dst = rs_d.at[i, pl.ds(*RS_PART[p]), :]
-        return remote(src, dst, rs_s.at[p, 15 + i], rs_r.at[p, 15 + i], near(d, HOP[i]))
+        return remote(src, dst, send.at[p, 8], rs_r.at[p, 15 + i], near(d, HOP[i]))
 
     for k in range(4):
-        for p in PARTS:
-            for i in range(3):
-                rs1(p, k, i).start()
+        own_second(rel("z", SUBSET[k]))
+        for i in range(3):
+            rs1(1, k, i).start()
+        if k < 3:
+            for m in range(4):
+                rs1(2, m, k).start()
+    for k in range(4):
+        for i in range(3):
+            rs1(0, k, i).start()
+    lax.fori_loop(0, 4, turn, 0)
     for k in range(4):
         for p in PARTS:
             rows = pl.ds(*RS_PART[p])
@@ -566,7 +592,7 @@
     for p in PARTS:
         rows = pl.ds(*RS_PART[p])
         for i in range(3):
-            rs2(p, i).wait_recv()
+            arrive(rs_c.at[i, :, rows, :], rs_r.at[p, 12 + i])
 
         def add_second(n, _, p=p, rows=rows):
             ref = own_ref(p, me[ORDER[p][0]], me[ORDER[p][1]], n)
@@ -583,16 +609,14 @@
     for p in PARTS:
         rows = pl.ds(*RS_PART[p])
         for i in range(3):
-            rs3(p, i).wait_recv()
+            arrive(rs_d.at[i, rows, :], rs_r.at[p, 15 + i])
         total = own_ref(p, *own_at(p))[...]
         for i in range(3):
             total = total + rs_d[i, rows, :].astype(F32)
         fin[rows, :] = total
 
     rows = slab(ph)
-    scale = scale_s[rows, :]
-    raw = s_rows[...].astype(F32)
-    gain = s_gain[...].astype(F32)
+    scale = scale_s[...]
     sums = []
     for h in range(2):
         sums.append(rowsum_tokens(fin[h * 64 : h * 64 + 64, :] * raw[:, h * 128 : h * 128 + 128] * scale))
@@ -608,25 +632,21 @@
     loss_out[...] = jnp.where(c == 1, window[:, 64:128], window[:, 0:64])
 
     for p in PARTS:
-        for i in range(3):
-            p1(p, i).wait_send()
-        for i in range(8):
-            p2(p, i // 2, i % 2).wait_send()
-        for i in range(2):
-            p2f(p, i).wait_send()
-        for i in range(4):
-            p3s(p, i).wait_send()
-        sib_s(p, c).wait_send()
-        for j in range(4):
-            for i in range(4):
-                p3t(p, j, i).wait_send()
-                sib_t(p, j, i).wait_send()
-        for i in range(3):
-            for k in range(4):
-                rs1(p, k, i).wait_send()
-            rs2(p, i).wait_send()
-            rs3(p, i).wait_send()
-    for ex in (early_tp, early_ph, late_tp, late_ph):
+        rows = pl.ds(*PART_T[p])
+        arrive(G.at[0, 0, 0, 0:3, rows, :], send.at[p, 0])
+        arrive(G.at[0, 0:3, 0, :, rows, :], send.at[p, 1])
+        arrive(G.at[0, 0:3, :, :, rows, :], send.at[p, 3])
+        arrive(G.at[0, :, :, :, rows, :], send.at[p, 4])
+        rows = pl.ds(*PART_S[p])
+        arrive(G.at[0, 0:3, :, :, rows, :], send.at[p, 2])
+        arrive(G.at[0, 0:3, 0:1, :, rows, :], send.at[p, 2])
+        arrive(G.at[0, 0, 0, 0:3, rows, :], send.at[p, 2])
+        arrive(G.at[0, :, :, :, rows, :], send.at[p, 5])
+        rows = pl.ds(*RS_PART[p])
+        arrive(rs_b.at[:, :, :, rows, :], send.at[p, 6])
+        arrive(rs_c.at[:, :, rows, :], send.at[p, 7])
+        arrive(rs_d.at[:, rows, :], send.at[p, 8])
+    for ex in (early_y, early_z, early_ph, late_tp, late_ph):
         ex[2]()
     ws_push.wait_send()
     gp_push.wait_send()
@@ -645,10 +665,32 @@
     return jnp.sum(value, axis=0, keepdims=True)
 
 
-def head_kernel(xst_ref, g_ref, out_ref):
-    out_ref[...] = jnp.dot(
-        xst_ref[...].reshape(512, TOKENS), g_ref[...], preferred_element_type=F32
-    ).astype(BF16)
+def head_kernel(
+    xst_hbm, g_hbm, loss_in, rows_in, gain_in, out_hbm, loss_out, rows_out, gain_out, xst, g, out, in_sem, out_sem
+):
+    g_load = pltpu.make_async_copy(g_hbm, g, in_sem.at[8])
+    g_load.start()
+    loads = [
+        pltpu.make_async_copy(xst_hbm.at[pl.ds(2 * i, 2)], xst.at[pl.ds(2 * i, 2)], in_sem.at[i]) for i in range(8)
+    ]
+    stores = [
+        pltpu.make_async_copy(out.at[pl.ds(512 * i, 512)], out_hbm.at[pl.ds(512 * i, 512)], out_sem.at[i])
+        for i in range(8)
+    ]
+    for load in loads:
+        load.start()
+    loss_out[...] = loss_in[...]
+    rows_out[...] = rows_in[...]
+    gain_out[...] = gain_in[...]
+    g_load.wait()
+    for i in range(8):
+        loads[i].wait()
+        out[512 * i : 512 * i + 512, :] = jnp.dot(
+            xst[2 * i : 2 * i + 2].reshape(512, TOKENS), g[...], preferred_element_type=F32
+        ).astype(BF16)
+        stores[i].start()
+    for store in stores:
+        store.wait()
 
 
 def local(teacher_rows, teacher_gain, teacher_head, student_rows, student_gain, student_head, labels):
@@ -671,7 +713,6 @@
             pltpu.VMEM((4, 2, 4, 4, 128, LOCAL_V), BF16),
             pltpu.VMEM((16, 256, LOCAL_V), BF16),
             pltpu.VMEM((16, 256, LOCAL_V), BF16),
-            pltpu.VMEM((16, TOKENS, 256), BF16),
             pltpu.VMEM((2, 256, TOKENS), BF16),
             pltpu.VMEM((TOKENS, LOCAL_V), F32),
             pltpu.VMEM((TOKENS, LOCAL_V), F32),
@@ -679,7 +720,7 @@
             pltpu.VMEM((TOKENS, 128), F32),
             pltpu.VMEM((TOKENS, 128), F32),
             pltpu.VMEM((TOKENS, 128), F32),
-            pltpu.VMEM((TOKENS, 1), F32),
+            pltpu.VMEM((SLAB, 1), F32),
             pltpu.VMEM((TOKENS, LOCAL_V), BF16),
             pltpu.VMEM((2, 256, LOCAL_V), BF16),
             pltpu.VMEM((256, LOCAL_V), BF16),
@@ -688,15 +729,15 @@
             pltpu.VMEM((3, 4, 128, 128), BF16),
             pltpu.VMEM((3, 128, 128), BF16),
             pltpu.VMEM((128, 128), F32),
-            pltpu.VMEM((16, 8, 128), F32),
+            pltpu.VMEM((4, 8, 128), F32),
+            pltpu.VMEM((4, 8, 128), F32),
             pltpu.VMEM((8, 8, 128), F32),
             pltpu.VMEM((16, 8, TOKENS), F32),
             pltpu.VMEM((8, 8, TOKENS), F32),
             pltpu.VMEM((8, 8, 256), F32),
-            dma((5,)), dma((3,)),
-            dma((3, 3)), dma((3, 3)), dma((3, 8)), dma((3, 8)), dma((3, 2)), dma((3, 2)),
-            dma((3, 4)), dma((3, 4)), dma((3, 16)), dma((3, 16)), dma((3,)), dma((3,)), dma((3, 16)), dma((3, 16)),
-            dma((5, 16)), dma((5, 16)), dma((2,)), dma((2,)), dma((3, 18)), dma((3, 18)),
+            dma((5,)), dma((3,)), dma((3, 9)),
+            dma((3, 3)), dma((3, 2)), dma((3, 2)), dma((3, 3)), dma((3, 3)), dma((3, 4)), dma((3, 16)),
+            dma((3,)), dma((3, 16)), dma((6,)), dma((6, 16)), dma((2,)), dma((2,)), dma((3, 18)),
         ],
         compiler_params=pltpu.CompilerParams(
             collective_id=0, has_side_effects=True, vmem_limit_bytes=63 << 20
@@ -711,17 +752,26 @@
         student_head.reshape(16, 256, LOCAL_V),
         labels.reshape(1, TOKENS),
     )
-    head_grad = pl.pallas_call(
+    head_grad, loss, rows_grad, gain_grad = pl.pallas_call(
         head_kernel,
-        grid=(8,),
-        out_shape=jax.ShapeDtypeStruct((DS, LOCAL_V), BF16),
-        in_specs=[
-            pl.BlockSpec((2, 256, TOKENS), lambda t: (t, 0, 0)),
-            pl.BlockSpec((TOKENS, LOCAL_V), lambda t: (0, 0)),
+        out_shape=(
+            jax.ShapeDtypeStruct((DS, LOCAL_V), BF16),
+            jax.ShapeDtypeStruct((1, SLAB), F32),
+            jax.ShapeDtypeStruct((SLAB, 256), BF16),
+            jax.ShapeDtypeStruct((1, 256), F32),
+        ),
+        in_specs=[hbm, hbm, vmem, vmem, vmem],
+        out_specs=(hbm, vmem, vmem, vmem),
+        scratch_shapes=[
+            pltpu.VMEM((16, 256, TOKENS), BF16),
+            pltpu.VMEM((TOKENS, LOCAL_V), BF16),
+            pltpu.VMEM((DS, LOCAL_V), BF16),
+            dma((9,)),
+            dma((8,)),
         ],
-        out_specs=pl.BlockSpec((512, LOCAL_V), lambda t: (t, 0)),
+        compiler_params=pltpu.CompilerParams(vmem_limit_bytes=32 << 20),
         name="head_grad",
-    )(xst, g)
+    )(xst, g, loss, rows_grad, gain_grad)
     return loss.reshape(SLAB), head_grad, rows_grad, gain_grad.reshape(256)
 
 

time: 130 us -> 114 us (0.88)
  Pallas kernels: 128 us -> 108 us
  local copies, waits for them, and re-layouts: 1.7 us -> 5.23 us
    pallas_call x1, Pallas kernels: 119 us -> 102 us  [local(): pl.pallas_call(comm_kernel, out_shape=(jax.ShapeDtypeStruct((1, SLAB), F3...]
    unnamed x9 -> x10, local copies, waits for them, and re-layouts: 1.7 us -> 5.23 us
    pallas_call x1, Pallas kernels: 8.19 us -> 5.4 us  [local(): pl.pallas_call(head_kernel, out_shape=(jax.ShapeDtypeStruct((DS, LOCAL_V)...]
where the time goes in v3:
time: 114 us
  Pallas kernels  108 us (95%)
  local copies, waits for them, and re-layouts  5.23 us (5%)
    pallas_call x1, Pallas kernels, local(): pl.pallas_call(comm_kernel, out_shape=(jax.ShapeDtypeStruct((1, SLAB), F3...  102 us
    pallas_call x1, Pallas kernels, local(): pl.pallas_call(head_kernel, out_shape=(jax.ShapeDtypeStruct((DS, LOCAL_V)...  5.4 us
    unnamed x10, local copies, waits for them, and re-layouts  5.23 us

profile of v3, /device:TPU:1, one launch (start us, length us, event | category | flops | bytes accessed | tf_op | source)
XLA Modules:
  0.0 113.5 jit_solution(17182053151310343547)
XLA Ops:
  0.6 102.3 %distill.1 = (f32[1,64]{1,0:T(1,128)}, bf16[64,256]{1,0:T(8,128)(2,1)}, f32[1,256]{1,0:T(1,128)}, bf16[16,256,512]{2,1,0:T(8,128)(2,1)}, bf16[512,512]{1,0:T(8,128)(2,1)}) custom-call(bf16[512,128]{1,0:T(8,128)(2,1)} %t_rows.1, bf16[1,128]{1,0:T(2,128)(2,1)} %bitcast.10, bf16[4,2,4,4,128,512]{5,4,3,2,1,0:T(8,128)(2,1)} %bitcast.7, bf16[64,256]{1,0:T(8,128)(2,1)} %s_rows.1, ...), custom_call_target="tpu_custom_call" | custom-call | tf_op jit(solution)/shard_map/distill/pallas_call | solution.py:700
  102.9 0.0 copy-start
  102.9 2.2 %copy-done = bf16[16,256,512]{2,1,0:T(8,128)(2,1)S(1)} copy-done((bf16[16,256,512]{2,1,0:T(8,128)(2,1)S(1)}, bf16[16,256,512]{2,1,0:T(8,128)(2,1)}, u32[]{:S(2)}) %copy-start) | copy-done | bytes 4194328
  105.1 0.0 copy-start.1
  105.1 1.0 copy-done.1
  106.1 0.0 copy-start.2
  106.1 0.8 copy-done.2
  106.9 0.0 copy-start.3
  106.9 0.7 copy-done.3
  107.6 0.0 copy-start.4
  107.6 0.6 copy-done.4
  108.1 5.4 %head_grad.1 = (bf16[4096,512]{1,0:T(8,128)(2,1)}, f32[1,64]{1,0:T(1,128)}, bf16[64,256]{1,0:T(8,128)(2,1)}, f32[1,256]{1,0:T(1,128)}) custom-call(bf16[16,256,512]{2,1,0:T(8,128)(2,1)S(1)} %copy-done, bf16[512,512]{1,0:T(8,128)(2,1)S(1)} %copy-done.1, f32[1,64]{1,0:T(1,128)S(1)} %copy-done.4, bf16[64,256]{1,0:T(8,128)(2,1)S(1)} %copy-done.2, ...), custom_call_target="tpu_custom_call" | custom-call | tf_op jit(solution)/shard_map/head_grad/pallas_call | solution.py:755
Async XLA Ops:
  102.9 2.2 %copy-start = (bf16[16,256,512]{2,1,0:T(8,128)(2,1)S(1)}, bf16[16,256,512]{2,1,0:T(8,128)(2,1)}, u32[]{:S(2)}) copy-start(bf16[16,256,512]{2,1,0:T(8,128)(2,1)} %get-tuple-element.13.xst_hbm) | copy-start | bytes 12582916
  105.1 1.0 copy-start.1
  106.1 0.8 copy-start.2
  106.9 0.7 copy-start.3
  107.6 0.6 copy-start.4

commit v4 on v3

--- a/solution.py
+++ b/solution.py
@@ -25,9 +25,9 @@
 
 def comm_kernel(
     t_rows, t_gain, wt_hbm, s_rows, s_gain, ws_hbm, labels,
-    loss_out, rows_out, gain_out, xst_out, g_out,
-    G, wt, ws, ws_sib, xst, acc_t, sl, es, st, col, lab, scale_s, g_ref, gp, gp_in, own,
-    rs_b, rs_c, rs_d, fin, ex_y0, ex_z0, ex_ph0, ex_tp1, ex_ph1, ex_gain,
+    loss_out, rows_out, gain_out, head_out,
+    G, wt, ws, ws_sib, head_part, acc_t, sl, es, st, col, lab, scale_s, g_ref, gp, gp_in, own,
+    rs_b, rs_c, rs_d, fin, ex_y0, ex_z0, ex_ph0, ex_tp1, ex_ph1, gain_col, gain_own, ex_gain, ex_gain_ph,
     w_sem, out_sem, send, r1, r2, r2f, r1s, r2s, r3s, r3t, sibs_r, sibt_r, ex_s, ex_r, misc_s, misc_r, rs_r,
 ):
     ph = lax.axis_index("phase")
@@ -206,7 +206,7 @@
     early_ph = exchange(ex_ph0, ph, 8, 1, to_ph)
     late_tp = exchange(ex_tp1, tp, 16, 2, to_tp)
     late_ph = exchange(ex_ph1, ph, 8, 3, to_ph)
-    gain_ph = exchange(ex_gain, ph, 8, 4, to_ph)
+    gain_ph = exchange(ex_gain_ph, ph, 8, 4, to_ph)
 
     def to_columns(rows):
         filled = jnp.concatenate(rows + [jnp.zeros((128 - len(rows), TOKENS), F32)], axis=0)
@@ -361,22 +361,27 @@
         lax.broadcasted_iota(jnp.int32, (256, 256), 0) == lax.broadcasted_iota(jnp.int32, (256, 256), 1)
     ).astype(F32).astype(BF16)
 
-    def xst_copy(t):
-        return pltpu.make_async_copy(xst.at[t % 2], xst_out.at[t], out_sem.at[t % 2])
-
-    def turn(z, _):
+    def head_copy(t):
+        return pltpu.make_async_copy(head_part.at[t % 2], head_out.at[t], out_sem.at[t % 2])
+
+    lane_c = lax.broadcasted_iota(jnp.int32, (256, 128), 1)
+
+    def head_layer(z, _):
         for y in range(4):
             t = 4 * z + y
             if y >= 2:
-                xst_copy(t - 2).wait()
+                head_copy(t - 2).wait()
             else:
 
                 @pl.when(z >= 1)
                 def _(t=t):
-                    xst_copy(t - 2).wait()
-
-            xst[t % 2] = nt_dot(eye, normed(z, y)).astype(BF16)
-            xst_copy(t).start()
+                    head_copy(t - 2).wait()
+
+            turned = nt_dot(eye, normed(z, y)).astype(BF16)
+            grad = jnp.dot(turned, g_ref[...], preferred_element_type=F32)
+            head_part[t % 2] = grad.astype(BF16)
+            head_copy(t).start()
+            gain_col[...] = jnp.where(lane_c == t, rowsum(grad * ws[t].astype(F32)), gain_col[...])
         return 0
 
     sl[...] = student_dot(0, 0)
@@ -489,8 +494,7 @@
         if which == 1:
             gp_push = remote(gp.at[1], gp_in, misc_s.at[1], misc_r.at[1], sib)
             gp_push.start()
-    g_copy = pltpu.make_async_copy(g_ref, g_out, out_sem.at[2])
-    g_copy.start()
+    gain_col[...] = jnp.zeros_like(gain_col)
 
     def own_first(z, _):
         for y in range(4):
@@ -567,8 +571,21 @@
     for k in range(4):
         for i in range(3):
             rs1(0, k, i).start()
-    lax.fori_loop(0, 4, turn, 0)
+    lax.fori_loop(0, 2, head_layer, 0)
+    def gain_copy(d):
+        to = (tp + d) % 16
+        return remote(gain_own.at[to], ex_gain.at[tp], misc_s.at[2], ex_r.at[6, d], (ph, to))
+
     for k in range(4):
+        if k in (1, 2):
+            lax.fori_loop(k + 1, k + 2, head_layer, 0)
+        if k == 2:
+            turned = jnp.transpose(gain_col[...])
+            for t in range(16):
+                gain_own[t] = jnp.broadcast_to(turned[t : t + 1], (8, 256))
+            ex_gain[tp] = gain_own[tp]
+            for d in range(1, 16):
+                gain_copy(d).start()
         for p in PARTS:
             rows = pl.ds(*RS_PART[p])
             for i in range(3):
@@ -606,6 +623,13 @@
         lax.fori_loop(0, 4, add_second, 0)
         for i in range(3):
             rs3(p, i).start()
+    for d in range(1, 16):
+        gain_copy(d).wait_recv()
+    total = ex_gain[0]
+    for i in range(1, 16):
+        total = total + ex_gain[i]
+    ex_gain_ph[ph] = total
+    gain_ph[0]()
     for p in PARTS:
         rows = pl.ds(*RS_PART[p])
         for i in range(3):
@@ -617,11 +641,6 @@
 
     rows = slab(ph)
     scale = scale_s[...]
-    sums = []
-    for h in range(2):
-        sums.append(rowsum_tokens(fin[h * 64 : h * 64 + 64, :] * raw[:, h * 128 : h * 128 + 128] * scale))
-    ex_gain[ph] = jnp.broadcast_to(jnp.concatenate(sums, axis=1), (8, 256))
-    gain_ph[0]()
     coefficient = scale * scale * col[rows, 2:3] / DS
     for h in range(2):
         cols = pl.ds(h * 128, 128)
@@ -650,45 +669,31 @@
         ex[2]()
     ws_push.wait_send()
     gp_push.wait_send()
-    xst_copy(14).wait()
-    xst_copy(15).wait()
-    g_copy.wait()
+    head_copy(14).wait()
+    head_copy(15).wait()
+    arrive(ex_gain.at[pl.ds(0, 15)], misc_s.at[2])
     gain_ph[1]()
-    total = ex_gain[0]
+    total = ex_gain_ph[0]
     for i in range(1, 8):
-        total = total + ex_gain[i]
-    gain_out[...] = total[0:1]
+        total = total + ex_gain_ph[i]
+    gain_out[...] = total[0:1] / jnp.concatenate([gain[0:1], gain[1:2]], axis=1)
     gain_ph[2]()
 
 
-def rowsum_tokens(value):
-    return jnp.sum(value, axis=0, keepdims=True)
-
-
-def head_kernel(
-    xst_hbm, g_hbm, loss_in, rows_in, gain_in, out_hbm, loss_out, rows_out, gain_out, xst, g, out, in_sem, out_sem
-):
-    g_load = pltpu.make_async_copy(g_hbm, g, in_sem.at[8])
-    g_load.start()
-    loads = [
-        pltpu.make_async_copy(xst_hbm.at[pl.ds(2 * i, 2)], xst.at[pl.ds(2 * i, 2)], in_sem.at[i]) for i in range(8)
-    ]
-    stores = [
-        pltpu.make_async_copy(out.at[pl.ds(512 * i, 512)], out_hbm.at[pl.ds(512 * i, 512)], out_sem.at[i])
-        for i in range(8)
-    ]
+def out_kernel(head_in, loss_in, rows_in, gain_in, head_out, loss_out, rows_out, gain_out, held, in_sem, out_sem):
+    def part(ref, i):
+        return ref.at[pl.ds(1024 * i, 1024)]
+
+    loads = [pltpu.make_async_copy(part(head_in, i), part(held, i), in_sem.at[i]) for i in range(4)]
+    stores = [pltpu.make_async_copy(part(held, i), part(head_out, i), out_sem.at[i]) for i in range(4)]
     for load in loads:
         load.start()
     loss_out[...] = loss_in[...]
     rows_out[...] = rows_in[...]
     gain_out[...] = gain_in[...]
-    g_load.wait()
-    for i in range(8):
-        loads[i].wait()
-        out[512 * i : 512 * i + 512, :] = jnp.dot(
-            xst[2 * i : 2 * i + 2].reshape(512, TOKENS), g[...], preferred_element_type=F32
-        ).astype(BF16)
-        stores[i].start()
+    for load, store in zip(loads, stores):
+        load.wait()
+        store.start()
     for store in stores:
         store.wait()
 
@@ -697,23 +702,22 @@
     vmem = pl.BlockSpec(memory_space=pltpu.VMEM)
     hbm = pl.BlockSpec(memory_space=pl.ANY)
     dma = pltpu.SemaphoreType.DMA
-    loss, rows_grad, gain_grad, xst, g = pl.pallas_call(
+    loss, rows_grad, gain_grad, head_grad = pl.pallas_call(
         comm_kernel,
         out_shape=(
             jax.ShapeDtypeStruct((1, SLAB), F32),
             jax.ShapeDtypeStruct((SLAB, 256), BF16),
             jax.ShapeDtypeStruct((1, 256), F32),
-            jax.ShapeDtypeStruct((16, 256, TOKENS), BF16),
-            jax.ShapeDtypeStruct((TOKENS, LOCAL_V), BF16),
+            jax.ShapeDtypeStruct((16, 256, LOCAL_V), BF16),
         ),
         in_specs=[vmem, vmem, hbm, vmem, vmem, hbm, vmem],
-        out_specs=(vmem, vmem, vmem, hbm, hbm),
+        out_specs=(vmem, vmem, vmem, hbm),
         scratch_shapes=[
             pltpu.VMEM((2, 4, 4, 4, 640, 128), BF16),
             pltpu.VMEM((4, 2, 4, 4, 128, LOCAL_V), BF16),
             pltpu.VMEM((16, 256, LOCAL_V), BF16),
             pltpu.VMEM((16, 256, LOCAL_V), BF16),
-            pltpu.VMEM((2, 256, TOKENS), BF16),
+            pltpu.VMEM((2, 256, LOCAL_V), BF16),
             pltpu.VMEM((TOKENS, LOCAL_V), F32),
             pltpu.VMEM((TOKENS, LOCAL_V), F32),
             pltpu.VMEM((TOKENS, LOCAL_V), F32),
@@ -734,10 +738,13 @@
             pltpu.VMEM((8, 8, 128), F32),
             pltpu.VMEM((16, 8, TOKENS), F32),
             pltpu.VMEM((8, 8, TOKENS), F32),
+            pltpu.VMEM((256, 128), F32),
+            pltpu.VMEM((16, 8, 256), F32),
+            pltpu.VMEM((16, 8, 256), F32),
             pltpu.VMEM((8, 8, 256), F32),
-            dma((5,)), dma((3,)), dma((3, 9)),
+            dma((5,)), dma((2,)), dma((3, 9)),
             dma((3, 3)), dma((3, 2)), dma((3, 2)), dma((3, 3)), dma((3, 3)), dma((3, 4)), dma((3, 16)),
-            dma((3,)), dma((3, 16)), dma((6,)), dma((6, 16)), dma((2,)), dma((2,)), dma((3, 18)),
+            dma((3,)), dma((3, 16)), dma((6,)), dma((7, 16)), dma((3,)), dma((2,)), dma((3, 18)),
         ],
         compiler_params=pltpu.CompilerParams(
             collective_id=0, has_side_effects=True, vmem_limit_bytes=63 << 20
@@ -753,25 +760,19 @@
         labels.reshape(1, TOKENS),
     )
     head_grad, loss, rows_grad, gain_grad = pl.pallas_call(
-        head_kernel,
+        out_kernel,
         out_shape=(
             jax.ShapeDtypeStruct((DS, LOCAL_V), BF16),
             jax.ShapeDtypeStruct((1, SLAB), F32),
             jax.ShapeDtypeStruct((SLAB, 256), BF16),
             jax.ShapeDtypeStruct((1, 256), F32),
         ),
-        in_specs=[hbm, hbm, vmem, vmem, vmem],
+        in_specs=[hbm, vmem, vmem, vmem],
         out_specs=(hbm, vmem, vmem, vmem),
-        scratch_shapes=[
-            pltpu.VMEM((16, 256, TOKENS), BF16),
-            pltpu.VMEM((TOKENS, LOCAL_V), BF16),
-            pltpu.VMEM((DS, LOCAL_V), BF16),
-            dma((9,)),
-            dma((8,)),
-        ],
-        compiler_params=pltpu.CompilerParams(vmem_limit_bytes=32 << 20),
-        name="head_grad",
-    )(xst, g, loss, rows_grad, gain_grad)
+        scratch_shapes=[pltpu.VMEM((DS, LOCAL_V), BF16), dma((4,)), dma((4,))],
+        compiler_params=pltpu.CompilerParams(vmem_limit_bytes=63 << 20),
+        name="outputs",
+    )(head_grad.reshape(DS, LOCAL_V), loss, rows_grad, gain_grad)
     return loss.reshape(SLAB), head_grad, rows_grad, gain_grad.reshape(256)
 
 

time: 114 us -> 107 us (0.939)
  local copies, waits for them, and re-layouts: 5.23 us -> 0 us
  Pallas kernels: 108 us -> 106 us
    unnamed x10 -> x0, local copies, waits for them, and re-layouts: 5.23 us -> none
where the time goes in v4:
time: 107 us
  Pallas kernels  106 us (99%)
    pallas_call x1, Pallas kernels, local(): pl.pallas_call(comm_kernel, out_shape=(jax.ShapeDtypeStruct((1, SLAB), F3...  101 us
    pallas_call x1, Pallas kernels, local(): pl.pallas_call(out_kernel, out_shape=(jax.ShapeDtypeStruct((DS, LOCAL_V),...  4.67 us

profile of v4, /device:TPU:1, one launch (start us, length us, event | category | flops | bytes accessed | tf_op | source)
XLA Modules:
  0.0 106.9 jit_solution(5010176698421788153)
XLA Ops:
  0.6 101.4 %distill.1 = (f32[1,64]{1,0:T(1,128)}, bf16[64,256]{1,0:T(8,128)(2,1)}, f32[1,256]{1,0:T(1,128)}, bf16[16,256,512]{2,1,0:T(8,128)(2,1)}) custom-call(bf16[512,128]{1,0:T(8,128)(2,1)} %t_rows.1, bf16[1,128]{1,0:T(2,128)(2,1)} %bitcast.12, bf16[4,2,4,4,128,512]{5,4,3,2,1,0:T(8,128)(2,1)} %bitcast.8, bf16[64,256]{1,0:T(8,128)(2,1)} %s_rows.1, ...), custom_call_target="tpu_custom_call" | custom-call | tf_op jit(solution)/shard_map/distill/pallas_call | solution.py:705
  102.1 4.7 %outputs.1 = (bf16[4096,512]{1,0:T(8,128)(2,1)}, f32[1,64]{1,0:T(1,128)}, bf16[64,256]{1,0:T(8,128)(2,1)}, f32[1,256]{1,0:T(1,128)}) custom-call(bf16[4096,512]{1,0:T(8,128)(2,1)} %bitcast.9, f32[1,64]{1,0:T(1,128)} %get-tuple-element.13.loss_in, bf16[64,256]{1,0:T(8,128)(2,1)} %get-tuple-element.14.rows_in, f32[1,256]{1,0:T(1,128)} %get-tuple-element.15.gain_in), custom_call_target="tpu_custom_call" | custom-call | tf_op jit(solution)/shard_map/outputs/pallas_call | solution.py:762

commit v5 on v4

--- a/solution.py
+++ b/solution.py
@@ -18,6 +18,7 @@
 PART_T = ((48, 160), (256, 160), (448, 192))
 TOKEN_T = (0, 160, 320)
 ORDER = (("x", "y", "z"), ("y", "z", "x"), ("z", "x", "y"))
+RS_ORDER = (("x", "z", "y"), ("y", "z", "x"), ("z", "x", "y"))
 RS_PART = ((0, 48), (48, 48), (96, 32))
 ALL = slice(None)
 LOW, HIGH = pl.ds(0, 2), pl.ds(2, 2)
@@ -401,7 +402,12 @@
             out = jnp.where(lane == first + i, column, out)
         return out
 
-    def student_stats(q, _):
+    def student_stats(n, _):
+        student_slab(2 * n)
+        student_slab(2 * n + 1)
+        return 0
+
+    def student_slab(q):
         rows = slab(q)
         logits = sl[rows, :]
         top = jnp.max(logits, axis=1, keepdims=True)
@@ -411,9 +417,8 @@
         st[rows, :] = pack(
             [top, rowsum(e), rowsum(e * logits), rowsum(picked)], 4, jnp.zeros((SLAB, 128), F32)
         )
-        return 0
-
-    lax.fori_loop(0, 8, student_stats, 0)
+
+    lax.fori_loop(0, 4, student_stats, 0)
     consume(2, 1)
     consume(2, 2)
     forward(3)
@@ -427,7 +432,12 @@
     sib_wait(3, 3)
     products(3, 3, 1 - c)
 
-    def teacher_stats(q, _):
+    def teacher_stats(n, _):
+        teacher_slab(2 * n)
+        teacher_slab(2 * n + 1)
+        return 0
+
+    def teacher_slab(q):
         rows = slab(q)
         logits = acc_t[rows, :] * col[rows, 0:1]
         student = sl[rows, :]
@@ -435,9 +445,8 @@
         e = jnp.exp(logits - top)
         acc_t[rows, :] = e
         st[rows, :] = pack([top, rowsum(e), rowsum(e * (logits - student)), rowsum(e * student)], 0, st[rows, :])
-        return 0
-
-    lax.fori_loop(0, 8, teacher_stats, 0)
+
+    lax.fori_loop(0, 4, teacher_stats, 0)
     stats = jnp.transpose(st[...])[0:8, :]
     sub = lax.broadcasted_iota(jnp.int32, (8, TOKENS), 0)
 
@@ -487,10 +496,11 @@
     for which in (1, 0):
 
         def grad_step(n, _, which=which):
-            logit_grad(n, which)
+            logit_grad(2 * n, which)
+            logit_grad(2 * n + 1, which)
             return 0
 
-        lax.fori_loop(0, 4, grad_step, 0)
+        lax.fori_loop(0, 2, grad_step, 0)
         if which == 1:
             gp_push = remote(gp.at[1], gp_in, misc_s.at[1], misc_r.at[1], sib)
             gp_push.start()
@@ -519,12 +529,12 @@
     gp_push.wait_recv()
 
     def at3(p, one, two, three):
-        a, b, d = ORDER[p]
+        a, b, d = RS_ORDER[p]
         at = {a: one, b: two, d: three}
         return at["x"], at["z"], at["y"]
 
     def rest(p, two, three):
-        at = {ORDER[p][1]: two, ORDER[p][2]: three}
+        at = {RS_ORDER[p][1]: two, RS_ORDER[p][2]: three}
         return tuple(at[axis] for axis in ("x", "z", "y") if axis in at)
 
     def stage_ref(p, one, two, three):
@@ -539,24 +549,24 @@
     SUBSET = (2, 1, -1, 0)
 
     def rs1(p, k, i):
-        a, b, d = ORDER[p]
+        a, b, d = RS_ORDER[p]
         two = rel(b, SUBSET[k])
         src = stage_ref(p, rel(a, HOP[i]), two, ALL)
         dst = rs_b.at[(i, *rest(p, two, ALL), pl.ds(*RS_PART[p]), ALL)]
         return remote(src, dst, send.at[p, 6], rs_r.at[p, 3 * k + i], near(a, HOP[i]))
 
     def rs1_wait(p, k, i):
-        dst = rs_b.at[(i, *rest(p, rel(ORDER[p][1], SUBSET[k]), ALL), pl.ds(*RS_PART[p]), ALL)]
+        dst = rs_b.at[(i, *rest(p, rel(RS_ORDER[p][1], SUBSET[k]), ALL), pl.ds(*RS_PART[p]), ALL)]
         arrive(dst, rs_r.at[p, 3 * k + i])
 
     def rs2(p, i):
-        a, b, d = ORDER[p]
+        a, b, d = RS_ORDER[p]
         src = stage_ref(p, me[a], rel(b, HOP[i]), ALL)
         dst = rs_c.at[i, :, pl.ds(*RS_PART[p]), :]
         return remote(src, dst, send.at[p, 7], rs_r.at[p, 12 + i], near(b, HOP[i]))
 
     def rs3(p, i):
-        a, b, d = ORDER[p]
+        a, b, d = RS_ORDER[p]
         src = stage_ref(p, me[a], me[b], rel(d, HOP[i]))
         dst = rs_d.at[i, pl.ds(*RS_PART[p]), :]
         return remote(src, dst, send.at[p, 8], rs_r.at[p, 15 + i], near(d, HOP[i]))
@@ -564,22 +574,18 @@
     for k in range(4):
         own_second(rel("z", SUBSET[k]))
         for i in range(3):
+            rs1(0, k, i).start()
             rs1(1, k, i).start()
         if k < 3:
             for m in range(4):
                 rs1(2, m, k).start()
-    for k in range(4):
-        for i in range(3):
-            rs1(0, k, i).start()
-    lax.fori_loop(0, 2, head_layer, 0)
     def gain_copy(d):
         to = (tp + d) % 16
         return remote(gain_own.at[to], ex_gain.at[tp], misc_s.at[2], ex_r.at[6, d], (ph, to))
 
     for k in range(4):
-        if k in (1, 2):
-            lax.fori_loop(k + 1, k + 2, head_layer, 0)
-        if k == 2:
+        lax.fori_loop(k, k + 1, head_layer, 0)
+        if k == 3:
             turned = jnp.transpose(gain_col[...])
             for t in range(16):
                 gain_own[t] = jnp.broadcast_to(turned[t : t + 1], (8, 256))
@@ -592,15 +598,15 @@
                 rs1_wait(p, k, i)
 
             def add_first(n, _, p=p, k=k, rows=rows):
-                two = rel(ORDER[p][1], SUBSET[k])
-                ref = own_ref(p, me[ORDER[p][0]], two, n)
+                two = rel(RS_ORDER[p][1], SUBSET[k])
+                ref = own_ref(p, me[RS_ORDER[p][0]], two, n)
                 total = ref[...]
                 for i in range(3):
                     total = total + rs_b[(i, *rest(p, two, n), rows, ALL)].astype(F32)
                 if k == 3:
                     ref[...] = total
                 else:
-                    stage_ref(p, me[ORDER[p][0]], two, n)[...] = total.astype(BF16)
+                    stage_ref(p, me[RS_ORDER[p][0]], two, n)[...] = total.astype(BF16)
                 return 0
 
             lax.fori_loop(0, 4, add_first, 0)
@@ -612,12 +618,12 @@
             arrive(rs_c.at[i, :, rows, :], rs_r.at[p, 12 + i])
 
         def add_second(n, _, p=p, rows=rows):
-            ref = own_ref(p, me[ORDER[p][0]], me[ORDER[p][1]], n)
+            ref = own_ref(p, me[RS_ORDER[p][0]], me[RS_ORDER[p][1]], n)
             total = ref[...]
             for i in range(3):
                 total = total + rs_c[i, n, rows, :].astype(F32)
             ref[...] = total
-            stage_ref(p, me[ORDER[p][0]], me[ORDER[p][1]], n)[...] = total.astype(BF16)
+            stage_ref(p, me[RS_ORDER[p][0]], me[RS_ORDER[p][1]], n)[...] = total.astype(BF16)
             return 0
 
         lax.fori_loop(0, 4, add_second, 0)
@@ -634,7 +640,7 @@
         rows = pl.ds(*RS_PART[p])
         for i in range(3):
             arrive(rs_d.at[i, rows, :], rs_r.at[p, 15 + i])
-        total = own_ref(p, *own_at(p))[...]
+        total = own_ref(p, *(me[axis] for axis in RS_ORDER[p]))[...]
         for i in range(3):
             total = total + rs_d[i, rows, :].astype(F32)
         fin[rows, :] = total
@@ -680,17 +686,19 @@
     gain_ph[2]()
 
 
-def out_kernel(head_in, loss_in, rows_in, gain_in, head_out, loss_out, rows_out, gain_out, held, in_sem, out_sem):
+def out_kernel(
+    head_in, loss_in, rows_in, gain_in, head_out, loss_out, rows_out, gain_out,
+    head, loss, rows, gain, in_sem, out_sem,
+):
     def part(ref, i):
         return ref.at[pl.ds(1024 * i, 1024)]
 
-    loads = [pltpu.make_async_copy(part(head_in, i), part(held, i), in_sem.at[i]) for i in range(4)]
-    stores = [pltpu.make_async_copy(part(held, i), part(head_out, i), out_sem.at[i]) for i in range(4)]
+    ways = [(part(head_in, i), part(head, i), part(head_out, i)) for i in range(4)]
+    ways += [(loss_in, loss, loss_out), (rows_in, rows, rows_out), (gain_in, gain, gain_out)]
+    loads = [pltpu.make_async_copy(src, held, in_sem.at[i]) for i, (src, held, _) in enumerate(ways)]
+    stores = [pltpu.make_async_copy(held, dst, out_sem.at[i]) for i, (_, held, dst) in enumerate(ways)]
     for load in loads:
         load.start()
-    loss_out[...] = loss_in[...]
-    rows_out[...] = rows_in[...]
-    gain_out[...] = gain_in[...]
     for load, store in zip(loads, stores):
         load.wait()
         store.start()
@@ -767,9 +775,16 @@
             jax.ShapeDtypeStruct((SLAB, 256), BF16),
             jax.ShapeDtypeStruct((1, 256), F32),
         ),
-        in_specs=[hbm, vmem, vmem, vmem],
-        out_specs=(hbm, vmem, vmem, vmem),
-        scratch_shapes=[pltpu.VMEM((DS, LOCAL_V), BF16), dma((4,)), dma((4,))],
+        in_specs=[hbm, hbm, hbm, hbm],
+        out_specs=(hbm, hbm, hbm, hbm),
+        scratch_shapes=[
+            pltpu.VMEM((DS, LOCAL_V), BF16),
+            pltpu.VMEM((1, SLAB), F32),
+            pltpu.VMEM((SLAB, 256), BF16),
+            pltpu.VMEM((1, 256), F32),
+            dma((7,)),
+            dma((7,)),
+        ],
         compiler_params=pltpu.CompilerParams(vmem_limit_bytes=63 << 20),
         name="outputs",
     )(head_grad.reshape(DS, LOCAL_V), loss, rows_grad, gain_grad)

time: 107 us -> 106 us (level)
    pallas_call x1, Pallas kernels: 4.67 us -> 3.36 us  [local(): pl.pallas_call(out_kernel, out_shape=(jax.ShapeDtypeStruct((DS, LOCAL_V),...]
where the time goes in v5:
time: 106 us
  Pallas kernels  105 us (99%)
    pallas_call x1, Pallas kernels, local(): pl.pallas_call(comm_kernel, out_shape=(jax.ShapeDtypeStruct((1, SLAB), F3...  102 us
    pallas_call x1, Pallas kernels, local(): pl.pallas_call(out_kernel, out_shape=(jax.ShapeDtypeStruct((DS, LOCAL_V),...  3.36 us

profile of v5, /device:TPU:1, one launch (start us, length us, event | category | flops | bytes accessed | tf_op | source)
XLA Modules:
  0.0 106.1 jit_solution(12037930224998032237)
XLA Ops:
  0.6 101.9 %distill.1 = (f32[1,64]{1,0:T(1,128)}, bf16[64,256]{1,0:T(8,128)(2,1)}, f32[1,256]{1,0:T(1,128)}, bf16[16,256,512]{2,1,0:T(8,128)(2,1)}) custom-call(bf16[512,128]{1,0:T(8,128)(2,1)} %t_rows.1, bf16[1,128]{1,0:T(2,128)(2,1)} %bitcast.12, bf16[4,2,4,4,128,512]{5,4,3,2,1,0:T(8,128)(2,1)} %bitcast.8, bf16[64,256]{1,0:T(8,128)(2,1)} %s_rows.1, ...), custom_call_target="tpu_custom_call" | custom-call | tf_op jit(solution)/shard_map/distill/pallas_call | solution.py:713
  102.5 3.4 %outputs.1 = (bf16[4096,512]{1,0:T(8,128)(2,1)}, f32[1,64]{1,0:T(1,128)}, bf16[64,256]{1,0:T(8,128)(2,1)}, f32[1,256]{1,0:T(1,128)}) custom-call(bf16[4096,512]{1,0:T(8,128)(2,1)} %bitcast.9, f32[1,64]{1,0:T(1,128)} %get-tuple-element.13.loss_in, bf16[64,256]{1,0:T(8,128)(2,1)} %get-tuple-element.14.rows_in, f32[1,256]{1,0:T(1,128)} %get-tuple-element.15.gain_in), custom_call_target="tpu_custom_call" | custom-call | tf_op jit(solution)/shard_map/outputs/pallas_call | solution.py:770

commit v6 on v5

--- a/solution.py
+++ b/solution.py
@@ -19,7 +19,7 @@
 TOKEN_T = (0, 160, 320)
 ORDER = (("x", "y", "z"), ("y", "z", "x"), ("z", "x", "y"))
 RS_ORDER = (("x", "z", "y"), ("y", "z", "x"), ("z", "x", "y"))
-RS_PART = ((0, 48), (48, 48), (96, 32))
+RS_PART = ((0, 48), (48, 48), (96, 48))
 ALL = slice(None)
 LOW, HIGH = pl.ds(0, 2), pl.ds(2, 2)
 
@@ -28,7 +28,7 @@
     t_rows, t_gain, wt_hbm, s_rows, s_gain, ws_hbm, labels,
     loss_out, rows_out, gain_out, head_out,
     G, wt, ws, ws_sib, head_part, acc_t, sl, es, st, col, lab, scale_s, g_ref, gp, gp_in, own,
-    rs_b, rs_c, rs_d, fin, ex_y0, ex_z0, ex_ph0, ex_tp1, ex_ph1, gain_col, gain_own, ex_gain, ex_gain_ph,
+    rs_b, rs_c, rs_d, fin, ex_y0, ex_z0, ex_ph0, ex_tp1, ex_ph1, gain_in,
     w_sem, out_sem, send, r1, r2, r2f, r1s, r2s, r3s, r3t, sibs_r, sibt_r, ex_s, ex_r, misc_s, misc_r, rs_r,
 ):
     ph = lax.axis_index("phase")
@@ -207,7 +207,6 @@
     early_ph = exchange(ex_ph0, ph, 8, 1, to_ph)
     late_tp = exchange(ex_tp1, tp, 16, 2, to_tp)
     late_ph = exchange(ex_ph1, ph, 8, 3, to_ph)
-    gain_ph = exchange(ex_gain_ph, ph, 8, 4, to_ph)
 
     def to_columns(rows):
         filled = jnp.concatenate(rows + [jnp.zeros((128 - len(rows), TOKENS), F32)], axis=0)
@@ -362,28 +361,30 @@
         lax.broadcasted_iota(jnp.int32, (256, 256), 0) == lax.broadcasted_iota(jnp.int32, (256, 256), 1)
     ).astype(F32).astype(BF16)
 
-    def head_copy(t):
-        return pltpu.make_async_copy(head_part.at[t % 2], head_out.at[t], out_sem.at[t % 2])
+    def head_copy(t, y):
+        return pltpu.make_async_copy(head_part.at[y % 2], head_out.at[t], out_sem.at[y % 2])
 
     lane_c = lax.broadcasted_iota(jnp.int32, (256, 128), 1)
 
-    def head_layer(z, _):
+    def head_layer(z, first):
+        sums = jnp.zeros((256, 128), F32)
         for y in range(4):
             t = 4 * z + y
-            if y >= 2:
-                head_copy(t - 2).wait()
-            else:
-
-                @pl.when(z >= 1)
-                def _(t=t):
-                    head_copy(t - 2).wait()
-
+            if y >= 2 or not first:
+                head_copy(t, y).wait()
             turned = nt_dot(eye, normed(z, y)).astype(BF16)
             grad = jnp.dot(turned, g_ref[...], preferred_element_type=F32)
-            head_part[t % 2] = grad.astype(BF16)
-            head_copy(t).start()
-            gain_col[...] = jnp.where(lane_c == t, rowsum(grad * ws[t].astype(F32)), gain_col[...])
-        return 0
+            head_part[y % 2] = grad.astype(BF16)
+            head_copy(t, y).start()
+            sums = jnp.where(lane_c == y, rowsum(grad * ws[t].astype(F32)), sums)
+        sums = jnp.transpose(sums)
+        for y in range(4):
+            band = jnp.concatenate(
+                [sums[y : y + 1, 0:128], sums[y : y + 1, 128:256], jnp.zeros((14, 128), F32)], axis=0
+            )
+            for xt in range(4):
+                own[xt, z, y, 128:144] = band
+                wt[xt, 0, z, y, 32:48, 128:256] = band.astype(BF16)
 
     sl[...] = student_dot(0, 0)
     sl[...] += student_dot(0, 1)
@@ -504,7 +505,6 @@
         if which == 1:
             gp_push = remote(gp.at[1], gp_in, misc_s.at[1], misc_r.at[1], sib)
             gp_push.start()
-    gain_col[...] = jnp.zeros_like(gain_col)
 
     def own_first(z, _):
         for y in range(4):
@@ -518,11 +518,13 @@
         for y in range(4):
             r = nt_dot(gp_in[...], ws_sib[4 * z + y])
             for xt in range(4):
-                for h in range(2):
-                    at = pl.ds(64 * h, 64)
-                    total = own[xt, z, y, at, :] + r[xt * 64 : xt * 64 + 64, 128 * h : 128 * h + 128]
-                    own[xt, z, y, at, :] = total
-                    wt[xt, 0, z, y, at, 0:128] = total.astype(BF16)
+                total = own[xt, z, y, 0:64] + r[xt * 64 : xt * 64 + 64, 0:128]
+                own[xt, z, y, 0:64] = total
+                wt[xt, 0, z, y, 0:64, 0:128] = total.astype(BF16)
+                total = own[xt, z, y, 64:128] + r[xt * 64 : xt * 64 + 64, 128:256]
+                own[xt, z, y, 64:128] = total
+                wt[xt, 0, z, y, 64:96, 0:128] = total[0:32].astype(BF16)
+                wt[xt, 0, z, y, 0:32, 128:256] = total[32:64].astype(BF16)
 
     lax.fori_loop(0, 4, own_first, 0)
     ws_push.wait_recv()
@@ -539,7 +541,8 @@
 
     def stage_ref(p, one, two, three):
         ix, iz, iy = at3(p, one, two, three)
-        return wt.at[ix, 0, iz, iy, pl.ds(*RS_PART[p]), pl.ds(0, 128)]
+        row, size = ((0, 48), (48, 48), (0, 48))[p]
+        return wt.at[ix, 0, iz, iy, pl.ds(row, size), pl.ds(128 if p == 2 else 0, 128)]
 
     def own_ref(p, one, two, three):
         ix, iz, iy = at3(p, one, two, three)
@@ -576,42 +579,39 @@
         for i in range(3):
             rs1(0, k, i).start()
             rs1(1, k, i).start()
+        head_layer(rel("z", SUBSET[k]), k == 0)
         if k < 3:
             for m in range(4):
                 rs1(2, m, k).start()
-    def gain_copy(d):
-        to = (tp + d) % 16
-        return remote(gain_own.at[to], ex_gain.at[tp], misc_s.at[2], ex_r.at[6, d], (ph, to))
-
+
+    def first_sum(p, k):
+        rows = pl.ds(*RS_PART[p])
+        for i in range(3):
+            rs1_wait(p, k, i)
+
+        def add_first(n, _):
+            two = rel(RS_ORDER[p][1], SUBSET[k])
+            ref = own_ref(p, me[RS_ORDER[p][0]], two, n)
+            total = ref[...]
+            for i in range(3):
+                total = total + rs_b[(i, *rest(p, two, n), rows, ALL)].astype(F32)
+            if k == 3:
+                ref[...] = total
+            else:
+                stage_ref(p, me[RS_ORDER[p][0]], two, n)[...] = total.astype(BF16)
+            return 0
+
+        lax.fori_loop(0, 4, add_first, 0)
+        if k < 3:
+            rs2(p, k).start()
+
+    for k in range(3):
+        first_sum(0, k)
+        first_sum(1, k)
     for k in range(4):
-        lax.fori_loop(k, k + 1, head_layer, 0)
-        if k == 3:
-            turned = jnp.transpose(gain_col[...])
-            for t in range(16):
-                gain_own[t] = jnp.broadcast_to(turned[t : t + 1], (8, 256))
-            ex_gain[tp] = gain_own[tp]
-            for d in range(1, 16):
-                gain_copy(d).start()
-        for p in PARTS:
-            rows = pl.ds(*RS_PART[p])
-            for i in range(3):
-                rs1_wait(p, k, i)
-
-            def add_first(n, _, p=p, k=k, rows=rows):
-                two = rel(RS_ORDER[p][1], SUBSET[k])
-                ref = own_ref(p, me[RS_ORDER[p][0]], two, n)
-                total = ref[...]
-                for i in range(3):
-                    total = total + rs_b[(i, *rest(p, two, n), rows, ALL)].astype(F32)
-                if k == 3:
-                    ref[...] = total
-                else:
-                    stage_ref(p, me[RS_ORDER[p][0]], two, n)[...] = total.astype(BF16)
-                return 0
-
-            lax.fori_loop(0, 4, add_first, 0)
-            if k < 3:
-                rs2(p, k).start()
+        first_sum(2, k)
+    first_sum(0, 3)
+    first_sum(1, 3)
     for p in PARTS:
         rows = pl.ds(*RS_PART[p])
         for i in range(3):
@@ -629,13 +629,6 @@
         lax.fori_loop(0, 4, add_second, 0)
         for i in range(3):
             rs3(p, i).start()
-    for d in range(1, 16):
-        gain_copy(d).wait_recv()
-    total = ex_gain[0]
-    for i in range(1, 16):
-        total = total + ex_gain[i]
-    ex_gain_ph[ph] = total
-    gain_ph[0]()
     for p in PARTS:
         rows = pl.ds(*RS_PART[p])
         for i in range(3):
@@ -645,6 +638,8 @@
             total = total + rs_d[i, rows, :].astype(F32)
         fin[rows, :] = total
 
+    gain_push = remote(fin.at[pl.ds(128, 8)], gain_in, misc_s.at[2], misc_r.at[2], sib)
+    gain_push.start()
     rows = slab(ph)
     scale = scale_s[...]
     coefficient = scale * scale * col[rows, 2:3] / DS
@@ -675,15 +670,12 @@
         ex[2]()
     ws_push.wait_send()
     gp_push.wait_send()
-    head_copy(14).wait()
-    head_copy(15).wait()
-    arrive(ex_gain.at[pl.ds(0, 15)], misc_s.at[2])
-    gain_ph[1]()
-    total = ex_gain_ph[0]
-    for i in range(1, 8):
-        total = total + ex_gain_ph[i]
-    gain_out[...] = total[0:1] / jnp.concatenate([gain[0:1], gain[1:2]], axis=1)
-    gain_ph[2]()
+    head_copy(14, 0).wait()
+    head_copy(15, 1).wait()
+    gain_push.wait_recv()
+    total = (fin[128:136, :] + gain_in[...])[0:2] / gain
+    gain_out[...] = jnp.concatenate([total[0:1], total[1:2]], axis=1)
+    gain_push.wait_send()
 
 
 def out_kernel(
@@ -736,23 +728,20 @@
             pltpu.VMEM((TOKENS, LOCAL_V), BF16),
             pltpu.VMEM((2, 256, LOCAL_V), BF16),
             pltpu.VMEM((256, LOCAL_V), BF16),
-            pltpu.VMEM((4, 4, 4, 128, 128), F32),
-            pltpu.VMEM((3, 4, 4, 128, 128), BF16),
-            pltpu.VMEM((3, 4, 128, 128), BF16),
-            pltpu.VMEM((3, 128, 128), BF16),
-            pltpu.VMEM((128, 128), F32),
+            pltpu.VMEM((4, 4, 4, 144, 128), F32),
+            pltpu.VMEM((3, 4, 4, 144, 128), BF16),
+            pltpu.VMEM((3, 4, 144, 128), BF16),
+            pltpu.VMEM((3, 144, 128), BF16),
+            pltpu.VMEM((144, 128), F32),
             pltpu.VMEM((4, 8, 128), F32),
             pltpu.VMEM((4, 8, 128), F32),
             pltpu.VMEM((8, 8, 128), F32),
             pltpu.VMEM((16, 8, TOKENS), F32),
             pltpu.VMEM((8, 8, TOKENS), F32),
-            pltpu.VMEM((256, 128), F32),
-            pltpu.VMEM((16, 8, 256), F32),
-            pltpu.VMEM((16, 8, 256), F32),
-            pltpu.VMEM((8, 8, 256), F32),
+            pltpu.VMEM((8, 128), F32),
             dma((5,)), dma((2,)), dma((3, 9)),
             dma((3, 3)), dma((3, 2)), dma((3, 2)), dma((3, 3)), dma((3, 3)), dma((3, 4)), dma((3, 16)),
-            dma((3,)), dma((3, 16)), dma((6,)), dma((7, 16)), dma((3,)), dma((2,)), dma((3, 18)),
+            dma((3,)), dma((3, 16)), dma((6,)), dma((6, 16)), dma((3,)), dma((3,)), dma((3, 18)),
         ],
         compiler_params=pltpu.CompilerParams(
             collective_id=0, has_side_effects=True, vmem_limit_bytes=63 << 20

time: 106 us -> 106 us (level)
  no operation moved by 1% of the time
where the time goes in v6:
time: 106 us
  Pallas kernels  106 us (100%)
    pallas_call x1, Pallas kernels, local(): pl.pallas_call(comm_kernel, out_shape=(jax.ShapeDtypeStruct((1, SLAB), F3...  102 us
    pallas_call x1, Pallas kernels, local(): pl.pallas_call(out_kernel, out_shape=(jax.ShapeDtypeStruct((DS, LOCAL_V),...  3.36 us

profile of v6, /device:TPU:1, one launch (start us, length us, event | category | flops | bytes accessed | tf_op | source)
XLA Modules:
  0.0 106.3 jit_solution(16939981765620705708)
XLA Ops:
  0.6 102.2 %distill.1 = (f32[1,64]{1,0:T(1,128)}, bf16[64,256]{1,0:T(8,128)(2,1)}, f32[1,256]{1,0:T(1,128)}, bf16[16,256,512]{2,1,0:T(8,128)(2,1)}) custom-call(bf16[512,128]{1,0:T(8,128)(2,1)} %t_rows.1, bf16[1,128]{1,0:T(2,128)(2,1)} %bitcast.12, bf16[4,2,4,4,128,512]{5,4,3,2,1,0:T(8,128)(2,1)} %bitcast.8, bf16[64,256]{1,0:T(8,128)(2,1)} %s_rows.1, ...), custom_call_target="tpu_custom_call" | custom-call | tf_op jit(solution)/shard_map/distill/pallas_call | solution.py:705
  102.8 3.4 %outputs.1 = (bf16[4096,512]{1,0:T(8,128)(2,1)}, f32[1,64]{1,0:T(1,128)}, bf16[64,256]{1,0:T(8,128)(2,1)}, f32[1,256]{1,0:T(1,128)}) custom-call(bf16[4096,512]{1,0:T(8,128)(2,1)} %bitcast.9, f32[1,64]{1,0:T(1,128)} %get-tuple-element.13.loss_in, bf16[64,256]{1,0:T(8,128)(2,1)} %get-tuple-element.14.rows_in, f32[1,256]{1,0:T(1,128)} %get-tuple-element.15.gain_in), custom_call_target="tpu_custom_call" | custom-call | tf_op jit(solution)/shard_map/outputs/pallas_call | solution.py:759

commit v7 on v5

--- a/solution.py
+++ b/solution.py
@@ -367,6 +367,13 @@
 
     lane_c = lax.broadcasted_iota(jnp.int32, (256, 128), 1)
 
+    def turn(z, _):
+        for y in range(4):
+            turned = nt_dot(eye, normed(z, y)).astype(BF16)
+            wt[0, 1, z, y] = turned[0:128]
+            wt[1, 1, z, y] = turned[128:256]
+        return 0
+
     def head_layer(z, _):
         for y in range(4):
             t = 4 * z + y
@@ -378,7 +385,7 @@
                 def _(t=t):
                     head_copy(t - 2).wait()
 
-            turned = nt_dot(eye, normed(z, y)).astype(BF16)
+            turned = jnp.concatenate([wt[0, 1, z, y], wt[1, 1, z, y]], axis=0)
             grad = jnp.dot(turned, g_ref[...], preferred_element_type=F32)
             head_part[t % 2] = grad.astype(BF16)
             head_copy(t).start()
@@ -463,9 +470,11 @@
 
     ex_tp1[tp] = stats
     late_tp[0]()
+    lax.fori_loop(0, 2, turn, 0)
     late_tp[1]()
     ex_ph1[ph] = merge(ex_tp1, 16)
     late_ph[0]()
+    lax.fori_loop(2, 4, turn, 0)
     late_ph[1]()
     late = merge(ex_ph1, 8)
     teacher_top, teacher_total, student_top, student_total = late[0:1], late[1:2], late[4:5], late[5:6]
@@ -584,8 +593,9 @@
         return remote(gain_own.at[to], ex_gain.at[tp], misc_s.at[2], ex_r.at[6, d], (ph, to))
 
     for k in range(4):
-        lax.fori_loop(k, k + 1, head_layer, 0)
-        if k == 3:
+        if k < 3:
+            lax.fori_loop((0, 2, 3)[k], (2, 3, 4)[k], head_layer, 0)
+        if k == 2:
             turned = jnp.transpose(gain_col[...])
             for t in range(16):
                 gain_own[t] = jnp.broadcast_to(turned[t : t + 1], (8, 256))

time: 106 us -> 103 us (0.972)
  Pallas kernels: 105 us -> 102 us
    pallas_call x1, Pallas kernels: 102 us -> 98.4 us  [local(): pl.pallas_call(comm_kernel, out_shape=(jax.ShapeDtypeStruct((1, SLAB), F3...]
where the time goes in v7:
time: 103 us; the launch traced here: 102 us
  Pallas kernels  102 us (99%)
    pallas_call x1, Pallas kernels, local(): pl.pallas_call(comm_kernel, out_shape=(jax.ShapeDtypeStruct((1, SLAB), F3...  98.4 us
    pallas_call x1, Pallas kernels, local(): pl.pallas_call(out_kernel, out_shape=(jax.ShapeDtypeStruct((DS, LOCAL_V),...  3.36 us

profile of v7, /device:TPU:1, one launch (start us, length us, event | category | flops | bytes accessed | tf_op | source)
XLA Modules:
  0.0 102.4 jit_solution(14002887112823071348)
XLA Ops:
  0.6 98.4 %distill.1 = (f32[1,64]{1,0:T(1,128)}, bf16[64,256]{1,0:T(8,128)(2,1)}, f32[1,256]{1,0:T(1,128)}, bf16[16,256,512]{2,1,0:T(8,128)(2,1)}) custom-call(bf16[512,128]{1,0:T(8,128)(2,1)} %t_rows.1, bf16[1,128]{1,0:T(2,128)(2,1)} %bitcast.12, bf16[4,2,4,4,128,512]{5,4,3,2,1,0:T(8,128)(2,1)} %bitcast.8, bf16[64,256]{1,0:T(8,128)(2,1)} %s_rows.1, ...), custom_call_target="tpu_custom_call" | custom-call | tf_op jit(solution)/shard_map/distill/pallas_call | solution.py:723
  99.0 3.4 %outputs.1 = (bf16[4096,512]{1,0:T(8,128)(2,1)}, f32[1,64]{1,0:T(1,128)}, bf16[64,256]{1,0:T(8,128)(2,1)}, f32[1,256]{1,0:T(1,128)}) custom-call(bf16[4096,512]{1,0:T(8,128)(2,1)} %bitcast.9, f32[1,64]{1,0:T(1,128)} %get-tuple-element.13.loss_in, bf16[64,256]{1,0:T(8,128)(2,1)} %get-tuple-element.14.rows_in, f32[1,256]{1,0:T(1,128)} %get-tuple-element.15.gain_in), custom_call_target="tpu_custom_call" | custom-call | tf_op jit(solution)/shard_map/outputs/pallas_call | solution.py:780

commit v8 on v7

--- a/solution.py
+++ b/solution.py
@@ -433,8 +433,8 @@
     opposite(2)
     consume(3, 1)
     consume(3, 2)
+    opposite(3)
     consume(2, 3)
-    opposite(3)
     products(3, 3, c)
     sib_wait(3, 3)
     products(3, 3, 1 - c)

time: 103 us -> 102 us (level)
  no operation moved by 1% of the time
where the time goes in v8:
time: 102 us
  Pallas kernels  101 us (99%)
    pallas_call x1, Pallas kernels, local(): pl.pallas_call(comm_kernel, out_shape=(jax.ShapeDtypeStruct((1, SLAB), F3...  97.6 us
    pallas_call x1, Pallas kernels, local(): pl.pallas_call(out_kernel, out_shape=(jax.ShapeDtypeStruct((DS, LOCAL_V),...  3.36 us

profile of v8, /device:TPU:1, one launch (start us, length us, event | category | flops | bytes accessed | tf_op | source)
XLA Modules:
  0.0 101.6 jit_solution(18360855780746029717)
XLA Ops:
  0.6 97.6 %distill.1 = (f32[1,64]{1,0:T(1,128)}, bf16[64,256]{1,0:T(8,128)(2,1)}, f32[1,256]{1,0:T(1,128)}, bf16[16,256,512]{2,1,0:T(8,128)(2,1)}) custom-call(bf16[512,128]{1,0:T(8,128)(2,1)} %t_rows.1, bf16[1,128]{1,0:T(2,128)(2,1)} %bitcast.12, bf16[4,2,4,4,128,512]{5,4,3,2,1,0:T(8,128)(2,1)} %bitcast.8, bf16[64,256]{1,0:T(8,128)(2,1)} %s_rows.1, ...), custom_call_target="tpu_custom_call" | custom-call | tf_op jit(solution)/shard_map/distill/pallas_call | solution.py:723
  98.2 3.4 %outputs.1 = (bf16[4096,512]{1,0:T(8,128)(2,1)}, f32[1,64]{1,0:T(1,128)}, bf16[64,256]{1,0:T(8,128)(2,1)}, f32[1,256]{1,0:T(1,128)}) custom-call(bf16[4096,512]{1,0:T(8,128)(2,1)} %bitcast.9, f32[1,64]{1,0:T(1,128)} %get-tuple-element.13.loss_in, bf16[64,256]{1,0:T(8,128)(2,1)} %get-tuple-element.14.rows_in, f32[1,256]{1,0:T(1,128)} %get-tuple-element.15.gain_in), custom_call_target="tpu_custom_call" | custom-call | tf_op jit(solution)/shard_map/outputs/pallas_call | solution.py:780
